TPU v7x, 32 devices: a whole 2x2x4 slice. The times are simulated.
32 devices in a mesh: dp: 16 (over z, y, core), blk: 2 (over x).
Axes of the slice: x: 2, y: 2, z: 4, core: 2. Of those that a mesh axis runs over, the one named last changes fastest.
Arguments:
- tokens: bfloat16 [256, 64, 768], P('blk', 'dp'), may hold values from -6 to 6
- timesteps: int32 [64], P('dp'), may hold values from 0 to 1999
- boundary: int32 [64], P('dp'), may hold values from 64 to 192
- importance: float32 [64], P('dp'), may hold values from 0.5 to 2
- cotangent: bfloat16 [256, 64, 768], P('blk', 'dp'), may hold values from -6 to 6
- time_weight: bfloat16 [128, 768], replicated, may hold values from -0.5 to 0.5
- time_bias: bfloat16 [768], replicated, may hold values from -3 to 3
- mixing_weight: bfloat16 [768, 2304], replicated, may hold values from -0.21875 to 0.21875
- query_bias: bfloat16 [768], replicated, may hold values from -2 to 2
- value_bias: bfloat16 [768], replicated, may hold values from -2 to 2
- output_weight: bfloat16 [768, 768], replicated, may hold values from -1.25 to 1.25
- output_bias: bfloat16 [768], replicated, may hold values from -2 to 2
- first_gain: bfloat16 [768], replicated, may hold values from 0.5 to 1.5
- first_shift: bfloat16 [768], replicated, may hold values from -2 to 2
- widen_weight: bfloat16 [768, 3072], replicated, may hold values from -0.21875 to 0.21875
- widen_bias: bfloat16 [3072], replicated, may hold values from -2 to 2
- narrow_weight: bfloat16 [3072, 768], replicated, may hold values from -0.15625 to 0.15625
- narrow_bias: bfloat16 [768], replicated, may hold values from -2 to 2
- second_gain: bfloat16 [768], replicated, may hold values from 0.5 to 1.5
- second_shift: bfloat16 [768], replicated, may hold values from -2 to 2
Outputs:
- output: bfloat16 [256, 64, 768], P('blk', 'dp')
- input_grad: bfloat16 [256, 64, 768], P('blk', 'dp')
- time_weight_grad: float32 [128, 768], replicated
- time_bias_grad: float32 [768], replicated
- mixing_weight_grad: float32 [768, 2304], replicated
- query_bias_grad: float32 [768], replicated
- value_bias_grad: float32 [768], replicated
- output_weight_grad: float32 [768, 768], replicated
- output_bias_grad: float32 [768], replicated
- first_gain_grad: float32 [768], replicated
- first_shift_grad: float32 [768], replicated
- expand_weight_grad: float32 [768, 3072], replicated
- expand_bias_grad: float32 [3072], replicated
- shrink_weight_grad: float32 [3072, 768], replicated
- shrink_bias_grad: float32 [768], replicated
- second_gain_grad: float32 [768], replicated
- second_shift_grad: float32 [768], replicated
All inputs are finite; a program needn't handle non-finite values.
Results may differ from a plain program's by a relative error of at most 0.023.
Values may be sent and summed in bfloat16 or wider, within the bound.
No kernel may reach another device: no remote copies, remote signals or barrier semaphores. Data moves between devices by JAX's collectives and lax.ppermute only.
A program may use at most 256 MiB of HBM per device.

v0:
```python
from functools import partial
import math

import jax
import jax.numpy as jnp
from jax import lax
from jax.sharding import PartitionSpec as P

HEADS = 12
HEAD = 64


epsilon = 1e-05


def sinusoid(step_ids, code_width):
    half_width = code_width // 2
    frequency = jnp.exp(-math.log(10000.0) * jnp.arange(half_width, dtype=jnp.float32) / half_width)
    angles = step_ids.astype(jnp.float32)[:, None] * frequency[None, :]
    return jnp.concatenate([jnp.cos(angles), jnp.sin(angles)], axis=-1)


def layer_norm(inputs, norm_gain, norm_shift):
    centred = inputs - jnp.mean(inputs, axis=-1, keepdims=True)
    variance = jnp.mean(centred * centred, axis=-1, keepdims=True)
    return centred * lax.rsqrt(variance + epsilon) * norm_gain + norm_shift


def reduce_dp(parts):
    shares = (
        lax.psum_scatter(
            parts[0].astype(jnp.bfloat16), "dp", scatter_dimension=1, tiled=True
        ).astype(jnp.float32),
        lax.psum_scatter(
            parts[1].astype(jnp.bfloat16), "dp", scatter_dimension=0, tiled=True
        ).astype(jnp.float32),
        lax.psum_scatter(
            parts[2].astype(jnp.bfloat16), "dp", scatter_dimension=0, tiled=True
        ).astype(jnp.float32),
        lax.psum_scatter(
            parts[3].astype(jnp.bfloat16), "dp", scatter_dimension=0, tiled=True
        ).astype(jnp.float32),
        lax.psum_scatter(
            parts[4].astype(jnp.bfloat16), "dp", scatter_dimension=0, tiled=True
        ).astype(jnp.float32),
        lax.psum_scatter(
            parts[5].astype(jnp.bfloat16), "dp", scatter_dimension=0, tiled=True
        ).astype(jnp.float32),
        lax.psum_scatter(
            parts[6].astype(jnp.bfloat16), "dp", scatter_dimension=0, tiled=True
        ).astype(jnp.float32),
        lax.psum_scatter(
            parts[7].astype(jnp.bfloat16), "dp", scatter_dimension=0, tiled=True
        ).astype(jnp.float32),
        lax.psum_scatter(
            parts[8].astype(jnp.bfloat16), "dp", scatter_dimension=0, tiled=True
        ).astype(jnp.float32),
        lax.psum_scatter(
            parts[9].astype(jnp.bfloat16), "dp", scatter_dimension=0, tiled=True
        ).astype(jnp.float32),
        lax.psum_scatter(
            parts[10].astype(jnp.bfloat16), "dp", scatter_dimension=0, tiled=True
        ).astype(jnp.float32),
        lax.psum_scatter(
            parts[11].astype(jnp.bfloat16), "dp", scatter_dimension=0, tiled=True
        ).astype(jnp.float32),
        lax.psum_scatter(
            parts[12].astype(jnp.bfloat16), "dp", scatter_dimension=0, tiled=True
        ).astype(jnp.float32),
        lax.psum_scatter(
            parts[13].astype(jnp.bfloat16), "dp", scatter_dimension=0, tiled=True
        ).astype(jnp.float32),
        lax.psum_scatter(
            parts[14].astype(jnp.bfloat16), "dp", scatter_dimension=0, tiled=True
        ).astype(jnp.float32),
    )
    summed = (
        lax.psum(shares[0].astype(jnp.bfloat16), "blk").astype(jnp.float32),
        lax.psum(shares[1].astype(jnp.bfloat16), "blk").astype(jnp.float32),
        lax.psum(shares[2].astype(jnp.bfloat16), "blk").astype(jnp.float32),
        lax.psum(shares[3].astype(jnp.bfloat16), "blk").astype(jnp.float32),
        lax.psum(shares[4].astype(jnp.bfloat16), "blk").astype(jnp.float32),
        lax.psum(shares[5].astype(jnp.bfloat16), "blk").astype(jnp.float32),
        lax.psum(shares[6].astype(jnp.bfloat16), "blk").astype(jnp.float32),
        lax.psum(shares[7].astype(jnp.bfloat16), "blk").astype(jnp.float32),
        lax.psum(shares[8].astype(jnp.bfloat16), "blk").astype(jnp.float32),
        lax.psum(shares[9].astype(jnp.bfloat16), "blk").astype(jnp.float32),
        lax.psum(shares[10].astype(jnp.bfloat16), "blk").astype(jnp.float32),
        lax.psum(shares[11].astype(jnp.bfloat16), "blk").astype(jnp.float32),
        lax.psum(shares[12].astype(jnp.bfloat16), "blk").astype(jnp.float32),
        lax.psum(shares[13].astype(jnp.bfloat16), "blk").astype(jnp.float32),
        lax.psum(shares[14].astype(jnp.bfloat16), "blk").astype(jnp.float32),
    )
    return (
        lax.all_gather(summed[0].astype(jnp.bfloat16), "dp", axis=1, tiled=True).astype(
            jnp.float32
        ),
        lax.all_gather(summed[1].astype(jnp.bfloat16), "dp", axis=0, tiled=True).astype(
            jnp.float32
        ),
        lax.all_gather(summed[2].astype(jnp.bfloat16), "dp", axis=0, tiled=True).astype(
            jnp.float32
        ),
        lax.all_gather(summed[3].astype(jnp.bfloat16), "dp", axis=0, tiled=True).astype(
            jnp.float32
        ),
        lax.all_gather(summed[4].astype(jnp.bfloat16), "dp", axis=0, tiled=True).astype(
            jnp.float32
        ),
        lax.all_gather(summed[5].astype(jnp.bfloat16), "dp", axis=0, tiled=True).astype(
            jnp.float32
        ),
        lax.all_gather(summed[6].astype(jnp.bfloat16), "dp", axis=0, tiled=True).astype(
            jnp.float32
        ),
        lax.all_gather(summed[7].astype(jnp.bfloat16), "dp", axis=0, tiled=True).astype(
            jnp.float32
        ),
        lax.all_gather(summed[8].astype(jnp.bfloat16), "dp", axis=0, tiled=True).astype(
            jnp.float32
        ),
        lax.all_gather(summed[9].astype(jnp.bfloat16), "dp", axis=0, tiled=True).astype(
            jnp.float32
        ),
        lax.all_gather(summed[10].astype(jnp.bfloat16), "dp", axis=0, tiled=True).astype(
            jnp.float32
        ),
        lax.all_gather(summed[11].astype(jnp.bfloat16), "dp", axis=0, tiled=True).astype(
            jnp.float32
        ),
        lax.all_gather(summed[12].astype(jnp.bfloat16), "dp", axis=0, tiled=True).astype(
            jnp.float32
        ),
        lax.all_gather(summed[13].astype(jnp.bfloat16), "dp", axis=0, tiled=True).astype(
            jnp.float32
        ),
        lax.all_gather(summed[14].astype(jnp.bfloat16), "dp", axis=0, tiled=True).astype(
            jnp.float32
        ),
    )


def shards(
    tokens,
    timesteps,
    boundary,
    importance,
    cotangent,
    time_weight,
    time_bias,
    mixing_weight,
    query_bias,
    value_bias,
    output_weight,
    output_bias,
    first_gain,
    first_shift,
    widen_weight,
    widen_bias,
    narrow_weight,
    narrow_bias,
    second_gain,
    second_shift,
):
    model_width = tokens.shape[2]
    score_scale = 1.0 / math.sqrt(HEAD)
    inputs, upstream = (tokens, cotangent)
    step_ids, bounds, weights = (timesteps, boundary, importance)
    offset = lax.axis_index("blk") * tokens.shape[0]
    row_count = inputs.shape[0]
    group_count = inputs.shape[1]
    time_code = sinusoid(step_ids, time_weight.shape[0]).astype(jnp.bfloat16)
    time_embed = jnp.dot(
        time_code, time_weight, preferred_element_type=jnp.float32
    ) + time_bias.astype(jnp.float32)
    hidden = inputs.astype(jnp.float32) + time_embed[None]
    hidden_low = hidden.astype(jnp.bfloat16)
    bias_pack = jnp.concatenate(
        [
            query_bias.astype(jnp.float32),
            jnp.zeros((model_width,), jnp.float32),
            value_bias.astype(jnp.float32),
        ]
    )
    packed = (
        jnp.einsum("lsd,de->lse", hidden_low, mixing_weight, preferred_element_type=jnp.float32)
        + bias_pack
    ).astype(jnp.bfloat16)
    queries = packed[..., :model_width].reshape(row_count, group_count, HEADS, HEAD)
    keys_values = packed[..., model_width:]
    both_all = lax.all_gather(keys_values, "blk", axis=0, tiled=True)
    total_rows = both_all.shape[0]
    keys_all = both_all[..., :model_width].reshape(total_rows, group_count, HEADS, HEAD)
    values_all = both_all[..., model_width:].reshape(total_rows, group_count, HEADS, HEAD)
    scores = (
        jnp.einsum("qshe,kshe->shqk", queries, keys_all, preferred_element_type=jnp.float32)
        * score_scale
    )
    row_peak = jnp.max(scores, axis=-1, keepdims=True)
    powered = jnp.exp(scores - row_peak)
    totals_soft = jnp.sum(powered, axis=-1, keepdims=True)
    probs_low = (powered / totals_soft).astype(jnp.bfloat16)
    log_total = row_peak + jnp.log(totals_soft)
    context = jnp.einsum(
        "shqk,kshe->qshe", probs_low, values_all, preferred_element_type=jnp.float32
    )
    context_low = context.reshape(row_count, group_count, model_width).astype(jnp.bfloat16)
    gain_one = first_gain.astype(jnp.float32)
    shift_one = first_shift.astype(jnp.float32)
    gain_two = second_gain.astype(jnp.float32)
    shift_two = second_shift.astype(jnp.float32)
    first_sum = (
        hidden
        + jnp.einsum("lsd,de->lse", context_low, output_weight, preferred_element_type=jnp.float32)
        + output_bias.astype(jnp.float32)
    )
    leading_norm, first_back = jax.vjp(layer_norm, first_sum, gain_one, shift_one)
    norm_reduced = leading_norm.astype(jnp.bfloat16)
    before_activation = jnp.einsum(
        "ikg,gv->ikv", norm_reduced, widen_weight, preferred_element_type=jnp.float32
    ) + widen_bias.astype(jnp.float32)
    activated, gelu_back = jax.vjp(partial(jax.nn.gelu, approximate=False), before_activation)
    activation_reduced = activated.astype(jnp.bfloat16)
    residual_sum = (
        leading_norm
        + jnp.einsum(
            "ema,aw->emw", activation_reduced, narrow_weight, preferred_element_type=jnp.float32
        )
        + narrow_bias.astype(jnp.float32)
    )
    out_full, second_back = jax.vjp(layer_norm, residual_sum, gain_two, shift_two)
    output = out_full.astype(jnp.bfloat16)
    positions = jnp.arange(row_count, dtype=jnp.int32) + offset
    row_weight = jnp.where(positions[:, None] >= bounds[None, :], weights[None, :], 0.0)
    out_grad = upstream.astype(jnp.float32) * row_weight[:, :, None]
    second_grad, second_gain_grad, second_shift_grad = second_back(out_grad)
    shrink_bias_grad = jnp.sum(second_grad, axis=(0, 1))
    narrow_reduced = second_grad.astype(jnp.bfloat16)
    shrink_weight_grad = jnp.einsum(
        "egk,egy->ky", activation_reduced, narrow_reduced, preferred_element_type=jnp.float32
    )
    act_grad = jnp.einsum(
        "ztv,ov->zto", narrow_reduced, narrow_weight, preferred_element_type=jnp.float32
    )
    pre_grad = gelu_back(act_grad)[0]
    expand_bias_grad = jnp.sum(pre_grad, axis=(0, 1))
    before_reduced = pre_grad.astype(jnp.bfloat16)
    expand_weight_grad = jnp.einsum(
        "thk,thr->kr", norm_reduced, before_reduced, preferred_element_type=jnp.float32
    )
    norm_grad = second_grad + jnp.einsum(
        "xcu,pu->xcp", before_reduced, widen_weight, preferred_element_type=jnp.float32
    )
    first_grad, first_gain_grad, first_shift_grad = first_back(norm_grad)
    output_bias_grad = jnp.sum(first_grad, axis=(0, 1))
    attn_low = first_grad.astype(jnp.bfloat16)
    output_weight_grad = jnp.einsum(
        "lsd,lse->de", context_low, attn_low, preferred_element_type=jnp.float32
    )
    context_grad = jnp.einsum(
        "lse,de->lsd", attn_low, output_weight, preferred_element_type=jnp.float32
    )
    context_grad = context_grad.astype(jnp.bfloat16).reshape(row_count, group_count, HEADS, HEAD)
    again = (
        jnp.einsum("qshe,kshe->shqk", queries, keys_all, preferred_element_type=jnp.float32)
        * score_scale
    )
    soft_probs = jnp.exp(again - log_total)
    prob_grad = jnp.einsum(
        "qshe,kshe->shqk", context_grad, values_all, preferred_element_type=jnp.float32
    )
    row_dot = jnp.sum(soft_probs * prob_grad, axis=-1, keepdims=True)
    score_low = (soft_probs * (prob_grad - row_dot)).astype(jnp.bfloat16)
    query_grad = (
        jnp.einsum("shqk,kshe->qshe", score_low, keys_all, preferred_element_type=jnp.float32)
        * score_scale
    )
    query_every, cgrad_every = (
        lax.all_gather(queries, "blk", axis=0, tiled=True),
        lax.all_gather(context_grad, "blk", axis=0, tiled=True),
    )
    total_every, dot_every = (
        lax.all_gather(log_total, "blk", axis=2, tiled=True),
        lax.all_gather(row_dot, "blk", axis=2, tiled=True),
    )
    own_keys = packed[..., model_width : 2 * model_width].reshape(
        row_count, group_count, HEADS, HEAD
    )
    own_values = packed[..., 2 * model_width :].reshape(row_count, group_count, HEADS, HEAD)
    local_scores = (
        jnp.einsum("qshe,kshe->shqk", query_every, own_keys, preferred_element_type=jnp.float32)
        * score_scale
    )
    local_probs = jnp.exp(local_scores - total_every)
    local_low = local_probs.astype(jnp.bfloat16)
    local_grad = jnp.einsum(
        "qshe,kshe->shqk", cgrad_every, own_values, preferred_element_type=jnp.float32
    )
    local_score_low = (local_probs * (local_grad - dot_every)).astype(jnp.bfloat16)
    value_own = jnp.einsum(
        "shqk,qshe->kshe", local_low, cgrad_every, preferred_element_type=jnp.float32
    )
    key_own = (
        jnp.einsum(
            "shqk,qshe->kshe", local_score_low, query_every, preferred_element_type=jnp.float32
        )
        * score_scale
    )
    key_here = jnp.concatenate(
        [
            key_own.reshape(row_count, group_count, model_width),
            value_own.reshape(row_count, group_count, model_width),
        ],
        axis=-1,
    )
    packed_grad = jnp.concatenate(
        [query_grad.reshape(row_count, group_count, model_width), key_here], axis=-1
    )
    query_bias_grad = jnp.sum(packed_grad[..., :model_width], axis=(0, 1))
    value_bias_grad = jnp.sum(packed_grad[..., 2 * model_width :], axis=(0, 1))
    packed_low = packed_grad.astype(jnp.bfloat16)
    mixing_weight_grad = jnp.einsum(
        "lsd,lse->de", hidden_low, packed_low, preferred_element_type=jnp.float32
    )
    hidden_grad = first_grad + jnp.einsum(
        "lse,de->lsd", packed_low, mixing_weight, preferred_element_type=jnp.float32
    )
    input_grad = hidden_grad.astype(jnp.bfloat16)
    time_total = jnp.sum(hidden_grad, axis=0)
    time_bias_grad = jnp.sum(time_total, axis=0)
    time_weight_grad = jnp.dot(
        time_code.astype(jnp.float32).T, time_total, precision=lax.Precision.HIGHEST
    )
    parts = (
        time_weight_grad,
        time_bias_grad,
        mixing_weight_grad,
        query_bias_grad,
        value_bias_grad,
        output_weight_grad,
        output_bias_grad,
        first_gain_grad,
        first_shift_grad,
        expand_weight_grad,
        expand_bias_grad,
        shrink_weight_grad,
        shrink_bias_grad,
        second_gain_grad,
        second_shift_grad,
    )
    summed = reduce_dp(parts)
    return (
        output,
        input_grad,
        summed[0],
        summed[1],
        summed[2],
        summed[3],
        summed[4],
        summed[5],
        summed[6],
        summed[7],
        summed[8],
        summed[9],
        summed[10],
        summed[11],
        summed[12],
        summed[13],
        summed[14],
    )


def solution(mesh):
    return jax.shard_map(
        shards,
        mesh=mesh,
        in_specs=(
            P("blk", "dp", None),
            P("dp"),
            P("dp"),
            P("dp"),
            P("blk", "dp", None),
            P(),
            P(),
            P(),
            P(),
            P(),
            P(),
            P(),
            P(),
            P(),
            P(),
            P(),
            P(),
            P(),
            P(),
            P(),
        ),
        out_specs=(
            P("blk", "dp", None),
            P("blk", "dp", None),
            P(),
            P(),
            P(),
            P(),
            P(),
            P(),
            P(),
            P(),
            P(),
            P(),
            P(),
            P(),
            P(),
            P(),
            P(),
        ),
        check_vma=False,
    )
```

profile of v0, /device:TPU:0, one launch (start us, length us, event | category | flops | bytes accessed | tf_op | source)
XLA Modules:
  0.0 767.1 jit_solution(12546675923529236721)
XLA Ops:
  35.0 30.8 %all-gather.10.cloned.1.call-done = bf16[256,4,1536]{2,0,1:T(8,128)(2,1)} async-done(((bf16[128,4,1536]{2,0,1:T(8,128)(2,1)}), bf16[256,4,1536]{2,0,1:T(8,128)(2,1)}) %all-gather.10.cloned.1.call-update) | async-done | bytes 3145744 | tf_op jit(solution)/shard_map/all_gather | solution.py:191
  72.1 6.1 multiply_reduce_fusion.1
  95.6 14.6 %multiply_convert_fusion.2 = (bf16[128,4,3072]{2,0,1:T(8,128)(2,1)S(1)}, f32[128,4,3072]{2,0,1:T(8,128)S(1)}) fusion(f32[128,4,3072]{2,0,1:T(8,128)S(1)} %get-tuple-element.134, f32[3072]{0:T(1024)S(1)} %convert_element_type.264, u8[128,3072]{1,0:T(8,128)(4,1)S(1)} %get-tuple-element.69, u8[128,3072]{1,0:T(8,128)(4,1)S(1)} %get-tuple-element.68), kind=kLoop, calls=%fused_computation.16 | loop fusion | flops 111673344 | bytes 16527360 | tf_op jit(solution)/shard_map/convert_element_type | solution.py:223
  117.1 9.7 %fusion.75 = (bf16[3072]{0:T(1024)(128)(2,1)}, bf16[128,4,3072]{2,0,1:T(8,128)(2,1)}) fusion(f32[128,4,3072]{2,0,1:T(8,128)S(1)} %get-tuple-element.118, bf16[3072,768]{1,0:T(8,128)(2,1)} %param.36, f32[128,4,768]{2,0,1:T(8,128)} %get-tuple-element.116, f32[128,4]{0,1:T(4,128)S(1)} %negate_multiply_fusion.2, f32[128,4,3072]{2,0,1:T(8,128)S(1)} %get-tuple-element.134, ...), kind=kOutput, calls=%fused_computation.129 | convolution fusion | flops 2441868288 | bytes 22040576 | tf_op jit(solution)/shard_map/ztv,ov->zto/dot_general | solution.py:242
  126.8 7.4 multiply_reduce_fusion.3
  148.5 9.2 %multiply_reduce_fusion = (f32[4,12,128]{2,1,0:T(8,128)}, f32[4,12,128,256]{3,2,1,0:T(8,128)}) fusion(f32[4,12,128,256]{3,2,1,0:T(8,128)} %get-tuple-element.131, f32[4,12,128]{2,1,0:T(8,128)} %log_add_fusion, bf16[128,4,12,64]{0,3,2,1:T(8,128)(2,1)} %bitcast.94, bf16[256,4,12,64]{0,3,2,1:T(8,128)(2,1)} %bitcast.98), kind=kOutput, calls=%fused_computation.13 | convolution fusion | flops 207611904 | bytes 14991360 | tf_op jit(solution)/shard_map/qshe,kshe->shqk/dot_general | solution.py:269
  157.7 7.3 bitcast_convert_fusion.5
  177.7 7.9 %multiply_convert_fusion.5 = bf16[4,12,64,128]{3,2,1,0:T(8,128)(2,1)} fusion(bf16[256,4,12,64]{0,3,2,1:T(8,128)(2,1)} %all-gather.12.cloned.1.call-done, f32[4,12,256,128]{3,2,1,0:T(8,128)} %fusion.76, f32[4,12,256]{2,1,0:T(8,128)} %all-gather.1, f32[4,12,256]{2,1,0:T(8,128)} %all-gather, bf16[256,4,12,64]{0,3,2,1:T(8,128)(2,1)} %all-gather.14.cloned.1.call-done, ...), kind=kOutput, calls=%fused_computation.64 | convolution fusion | flops 411303936 | bytes 11108352 | tf_op jit(solution)/shard_map/shqk,qshe->kshe/dot_general | solution.py:304
  188.0 6.0 bitcast_convert_fusion.4
  196.3 5.7 bitcast_convert_fusion.2
  202.4 7.3 bitcast_convert_fusion
  210.4 7.4 bitcast_convert_fusion.1
  218.0 11.0 %reduce-scatter.10.cloned.1.call-done = bf16[48,768]{1,0:T(8,128)(2,1)} async-done(((bf16[768,768]{1,0:T(8,128)(2,1)}), bf16[48,768]{1,0:T(8,128)(2,1)}) %reduce-scatter.10.cloned.1.call-update) | async-done | bytes 73744 | tf_op jit(solution)/shard_map/reduce_scatter | solution.py:46
  229.0 71.4 %reduce-scatter.8.cloned.1.call-done = bf16[48,2304]{1,0:T(8,128)(2,1)} async-done(((bf16[768,2304]{1,0:T(8,128)(2,1)}), bf16[48,2304]{1,0:T(8,128)(2,1)}) %reduce-scatter.8.cloned.1.call-update) | async-done | bytes 221200 | tf_op jit(solution)/shard_map/reduce_scatter | solution.py:37
  300.3 78.7 %reduce-scatter.14.cloned.1.call-done = bf16[192,768]{1,0:T(8,128)(2,1)} async-done(((bf16[3072,768]{1,0:T(8,128)(2,1)}), bf16[192,768]{1,0:T(8,128)(2,1)}) %reduce-scatter.14.cloned.1.call-update) | async-done | bytes 294928 | tf_op jit(solution)/shard_map/reduce_scatter | solution.py:64
  379.0 79.6 %reduce-scatter.12.cloned.1.call-done = bf16[48,3072]{1,0:T(8,128)(2,1)} async-done(((bf16[768,3072]{1,0:T(8,128)(2,1)}), bf16[48,3072]{1,0:T(8,128)(2,1)}) %reduce-scatter.12.cloned.1.call-update) | async-done | bytes 294928 | tf_op jit(solution)/shard_map/reduce_scatter | solution.py:58
  465.6 31.6 %all-reduce.26.cloned.1.call-done = (bf16[48,2304]{1,0:T(8,128)(2,1)}, bf16[48,768]{1,0:T(8,128)(2,1)}, bf16[48,3072]{1,0:T(8,128)(2,1)}, bf16[192,768]{1,0:T(8,128)(2,1)}) async-done(((bf16[48,2304]{1,0:T(8,128)(2,1)}, bf16[48,768]{1,0:T(8,128)(2,1)}, bf16[48,3072]{1,0:T(8,128)(2,1)}, bf16[192,768]{1,0:T(8,128)(2,1)}), (bf16[48,2304]{1,0:T(8,128)(2,1)}, bf16[48,768]{1,0:T(8,128)(2,1)}, ...) | async-done | bytes 884752 | tf_op jit(solution)/shard_map/psum | solution.py:80
  511.4 61.2 %all-reduce.21 = (bf16[768]{0:T(1024)(128)(2,1)}, bf16[768]{0:T(1024)(128)(2,1)}, bf16[768]{0:T(1024)(128)(2,1)}, bf16[768]{0:T(1024)(128)(2,1)}, bf16[768]{0:T(...) all-reduce(bf16[768]{0:T(1024)(128)(2,1)} %get-tuple-element.75, ...), channel_id=5, replica_groups=mesh['dp'=16,'blk'=2] {'dp'}, use_global_device_ids=true, to_apply=%region_15.16.clone | all-reduce | flops 9984 | bytes 39936
  585.9 8.8 %all-reduce.22 = (bf16[128,48]{0,1:T(8,128)(2,1)}, bf16[48]{0:T(256)(128)(2,1)}, bf16[48]{0:T(256)(128)(2,1)}, bf16[48]{0:T(256)(128)(2,1)}, bf16[48]{0:T(256)(1...) all-reduce(bf16[128,48]{0,1:T(8,128)(2,1)} %reduce-scatter.6.cloned, ...), channel_id=1, replica_groups=mesh['dp'=16,'blk'=2] {'blk'}, use_global_device_ids=true, to_apply=%region_13.14 | all-reduce | flops 6768 | bytes 27072 | tf_op jit(solution)/shard_map/psum | solution.py:78
  607.5 58.4 %all-reduce.20 = (bf16[768]{0:T(1024)(128)(2,1)}, bf16[768]{0:T(1024)(128)(2,1)}, bf16[768]{0:T(1024)(128)(2,1)}, bf16[768]{0:T(1024)(128)(2,1)}, bf16[768]{0:T(...) all-reduce(bf16[768]{0:T(1024)(128)(2,1)S(1)} %dynamic-update-slice, ...), channel_id=1, replica_groups=mesh['dp'=16,'blk'=2] {'dp'}, use_global_device_ids=true, to_apply=%add | all-reduce | flops 9984 | bytes 39936
  678.7 20.0 %all_gather.65 = bf16[128,768]{0,1:T(8,128)(2,1)} all-gather(bf16[128,48]{0,1:T(8,128)(2,1)} %get-tuple-element.98), channel_id=1, replica_groups=mesh['dp'=16,'blk'=2] {'dp'}, dimensions={1}, use_global_device_ids=true | all-gather | bytes 208896 | tf_op jit(solution)/shard_map/all_gather | solution.py:95
  708.8 7.4 convert_element_type.300
  716.2 37.4 %all-gather.22.cloned.1.call-done = bf16[3072,768]{1,0:T(8,128)(2,1)} async-done(((bf16[192,768]{1,0:T(8,128)(2,1)}), bf16[3072,768]{1,0:T(8,128)(2,1)}) %all-gather.22.cloned.1.call-update) | async-done | bytes 4718608 | tf_op jit(solution)/shard_map/all_gather | solution.py:128
  753.6 6.8 convert_element_type.304
  (254 shorter events, 158.1 us)
Async XLA Ops:
  7.2 58.6 %all-gather.10.cloned.1.call-start = ((), (), s32[]{:S(2)}) async-start(), calls=%async_computation.5 | async-start | bytes 4718592 | tf_op jit(solution)/shard_map/all_gather | solution.py:191
  18.1 122.3 %all-gather.12.cloned.1.call-start = ((), (), s32[]{:S(2)}) async-start(), calls=%async_computation.6 | async-start | bytes 2359296 | tf_op jit(solution)/shard_map/all_gather | solution.py:279
  23.5 154.2 %all-gather.14.cloned.1.call-start = ((), (), s32[]{:S(2)}) async-start(), calls=%async_computation.7 | async-start | bytes 2359296 | tf_op jit(solution)/shard_map/all_gather | solution.py:280
  90.6 43.6 %copy-start.2 = (f32[128,4,768]{2,0,1:T(8,128)}, f32[128,4,768]{2,0,1:T(8,128)S(1)}, u32[]{:S(2)}) copy-start(f32[128,4,768]{2,0,1:T(8,128)S(1)} %get-tuple-element.133) | copy-start | bytes 4718596
  90.7 43.6 %copy-start.22 = (f32[128,4]{0,1:T(4,128)}, f32[128,4]{0,1:T(4,128)S(1)}, u32[]{:S(2)}) copy-start(f32[128,4]{0,1:T(4,128)S(1)} %broadcast_multiply_fusion.1) | copy-start | bytes 6148
  90.7 19.6 %slice-start = ((s8[4718592]{0:T(1024)(128)(4,1)}), s8[4194304]{0:T(1024)(128)(4,1)S(1)}, s32[]{:S(2)}) async-start(s8[4718592]{0:T(1024)(128)(4,1)} %bitcast.106), calls=%async_computation.18 | async-start | bytes 8388608
  91.0 43.2 %copy-start.37 = (f32[128,4]{0,1:T(4,128)}, f32[128,4]{0,1:T(4,128)S(1)}, u32[]{:S(2)}) copy-start(f32[128,4]{0,1:T(4,128)S(1)} %fusion.58) | copy-start | bytes 6148
  91.1 19.2 %slice-start.1 = ((s8[4718592]{0:T(1024)(128)(4,1)}), s8[524288]{0:T(1024)(128)(4,1)S(1)}, s32[]{:S(2)}) async-start(s8[4718592]{0:T(1024)(128)(4,1)} %bitcast.106), calls=%async_computation.19 | async-start | bytes 1048576
  95.6 14.7 %copy-start.44 = (f32[768]{0:T(1024)S(1)}, f32[768]{0:T(1024)}, u32[]{:S(2)}) copy-start(f32[768]{0:T(1024)} %convert_element_type.266) | copy-start | bytes 9220
  117.1 85.3 %copy-start.34 = (f32[128,4]{0,1:T(4,128)}, f32[128,4]{0,1:T(4,128)S(1)}, u32[]{:S(2)}) copy-start(f32[128,4]{0,1:T(4,128)S(1)} %negate_multiply_fusion.2) | copy-start | bytes 6148
  134.9 11.6 %copy-start.35 = (f32[128,4]{0,1:T(4,128)}, f32[128,4]{0,1:T(4,128)S(1)}, u32[]{:S(2)}) copy-start(f32[128,4]{0,1:T(4,128)S(1)} %negate_multiply_fusion.1) | copy-start | bytes 6148
  140.1 88.9 %reduce-scatter.10.cloned.1.call-start = ((), (), s32[]{:S(2)}) async-start(), calls=%async_computation.11 | async-start | bytes 1253376 | tf_op jit(solution)/shard_map/reduce_scatter | solution.py:46
  157.7 142.7 %reduce-scatter.8.cloned.1.call-start = ((), (), s32[]{:S(2)}) async-start(), calls=%async_computation.9 | async-start | bytes 3760128 | tf_op jit(solution)/shard_map/reduce_scatter | solution.py:37
  202.0 177.1 %reduce-scatter.14.cloned.1.call-start = ((), (), s32[]{:S(2)}) async-start(), calls=%async_computation.15 | async-start | bytes 5013504 | tf_op jit(solution)/shard_map/reduce_scatter | solution.py:64
  209.8 248.8 %reduce-scatter.12.cloned.1.call-start = ((), (), s32[]{:S(2)}) async-start(), calls=%async_computation.13 | async-start | bytes 5013504 | tf_op jit(solution)/shard_map/reduce_scatter | solution.py:58
  217.9 240.8 %copy-start.36 = (f32[128,4]{0,1:T(4,128)S(1)}, f32[128,4]{0,1:T(4,128)}, u32[]{:S(2)}) copy-start(f32[128,4]{0,1:T(4,128)} %copy-done.35) | copy-start | bytes 6148
  217.9 279.3 %all-reduce.26.cloned.1.call-start = ((), (), s32[]{:S(2)}) async-start(), calls=%async_computation.17 | async-start | bytes 1769472 | tf_op jit(solution)/shard_map/psum | solution.py:80
  458.6 40.7 %copy-start.48 = (u32[32]{0:T(128)S(1)}, u32[32]{0:T(128)}, u32[]{:S(2)}) copy-start(u32[32]{0:T(128)} %constant.102) | copy-start | bytes 388
  458.6 127.3 %reduce-scatter.6.cloned.1.call-start = ((), (), s32[]{:S(2)}) async-start(), calls=%async_computation.8 | async-start | bytes 208896 | tf_op jit(solution)/shard_map/reduce_scatter | solution.py:31
  465.5 234.9 %all-gather.18.cloned.1.call-start = ((), (), s32[]{:S(2)}) async-start(), calls=%async_computation.12 | async-start | bytes 1253376 | tf_op jit(solution)/shard_map/all_gather | solution.py:110
  497.2 206.1 %all-gather.16.cloned.1.call-start = ((), (), s32[]{:S(2)}) async-start(), calls=%async_computation.10 | async-start | bytes 3760128 | tf_op jit(solution)/shard_map/all_gather | solution.py:101
  497.9 210.9 %all-gather.20.cloned.1.call-start = ((), (), s32[]{:S(2)}) async-start(), calls=%async_computation.14 | async-start | bytes 5013504 | tf_op jit(solution)/shard_map/all_gather | solution.py:122
  498.5 255.1 %all-gather.22.cloned.1.call-start = ((), (), s32[]{:S(2)}) async-start(), calls=%async_computation.16 | async-start | bytes 5013504 | tf_op jit(solution)/shard_map/all_gather | solution.py:128
  596.4 10.2 %copy-start.39 = (bf16[768]{0:T(1024)(128)(2,1)}, bf16[768]{0:T(1024)(128)(2,1)S(1)}, u32[]{:S(2)}) copy-start(bf16[768]{0:T(1024)(128)(2,1)S(1)} %dynamic-update-slice.1) | copy-start | bytes 4612
  (45 other events, 193.3 us)
Sparse Core Ops, SparseCore 0:
  18.1 47.6 all-gather.9
  67.9 27.1 all-gather.11
  140.2 27.1 all-gather.13
  170.9 58.0 reduce-scatter.9
  233.3 67.0 reduce-scatter.7
  304.6 74.3 reduce-scatter.13
  383.9 74.5 reduce-scatter.11
  461.1 36.0 all-reduce.25
  501.2 53.5 reduce-scatter.5
  557.0 37.4 all-gather.17
  596.7 46.5 all-gather.15
  645.5 53.7 all-gather.19
  701.5 52.0 all-gather.21
where the time goes:
time: 772 us; the launch traced here: 767 us
  waiting for transfers between devices  343 us (44%)
  blocking collectives  159 us (21%)
  matrix products  107 us (14%)
  other arithmetic  73.9 us (10%)
  local copies, waits for them, and re-layouts  66.2 us (9%)
  between operations  17.4 us (2%)
    unnamed x2, blocking collectives  120 us
    reduce_scatter x1, waiting for transfers between devices, reduce_dp(): lax.psum_scatter(parts[9].astype(jnp.bfloat16), 'dp', scatter_dimension=0...  79.6 us
    reduce_scatter x1, waiting for transfers between devices, reduce_dp(): lax.psum_scatter(parts[11].astype(jnp.bfloat16), 'dp', scatter_dimension=...  78.7 us
    reduce_scatter x1, waiting for transfers between devices, reduce_dp(): lax.psum_scatter(parts[2].astype(jnp.bfloat16), 'dp', scatter_dimension=0...  71.4 us
    all_gather x1, waiting for transfers between devices, reduce_dp(): lax.all_gather(summed[11].astype(jnp.bfloat16), 'dp', axis=0, tiled=True)  37.4 us
    unnamed x146, local copies, waits for them, and re-layouts  35.4 us
    psum x1, waiting for transfers between devices, reduce_dp(): lax.psum(shares[2].astype(jnp.bfloat16), 'blk').astype(jnp.float32)  31.6 us
    all_gather x1, waiting for transfers between devices, shards(): both_all = lax.all_gather(keys_values, 'blk', axis=0, tiled=True)  30.8 us
  transfers between devices with their start and end apart: 13, of which 7 were waited for; matrix products, arithmetic and copies ran while one was open for 30% of the time, Pallas kernels for 0%

commit v1 on v0

--- a/solution.py
+++ b/solution.py
@@ -4,6 +4,8 @@
 import jax
 import jax.numpy as jnp
 from jax import lax
+from jax.experimental import pallas as pl
+from jax.experimental.pallas import tpu as pltpu
 from jax.sharding import PartitionSpec as P
 
 HEADS = 12
@@ -140,7 +142,7 @@
     )
 
 
-def shards(
+def general_shards(
     tokens,
     timesteps,
     boundary,
@@ -370,9 +372,1074 @@
     )
 
 
+LOW = jnp.bfloat16
+FULL = jnp.float32
+PLACES = {"c": ("dp", 1), "y": ("dp", 2), "z": ("dp", 4), "w": ("dp", 8), "x": ("blk", 1)}
+SHRINK_ORDERS = ("xyz", "yxz")
+EXPAND_ORDERS = ("xyz", "yzx", "zxy")
+MIXING_ORDERS = ("xyz", "yzx", "zxy")
+ALL_ORDERS = ("xyz", "yxz", "yzx", "zxy")
+CORE, SIDE, NUMBERS = 0, 1, 2
+WIDTH = 768
+GRAD_ROWS = 3072
+
+
+def swap(value, place):
+    axis, bit = PLACES[place]
+    count = lax.axis_size(axis)
+    return lax.ppermute(value, axis, [(i, i ^ bit) for i in range(count)])
+
+
+def place_bit(place):
+    axis, bit = PLACES[place]
+    return (lax.axis_index(axis) // bit) % 2
+
+
+def device_info():
+    core = place_bit("c")
+    numbers = []
+    for order in ALL_ORDERS:
+        number = core
+        for place in order:
+            number = number * 2 + place_bit(place)
+        numbers.append(number)
+    return jnp.stack([core, lax.axis_index("blk")] + numbers).astype(jnp.int32)
+
+
+def order_number(info_ref, orders, unit):
+    number = info_ref[NUMBERS + ALL_ORDERS.index(orders[0])]
+    for k in range(1, len(orders)):
+        number = jnp.where(unit == k, info_ref[NUMBERS + ALL_ORDERS.index(orders[k])], number)
+    return number
+
+
+def weight_half(left, right, info, orders, left_of, right_of, got=None):
+    units = len(orders)
+    block = GRAD_ROWS // units // 16
+    tile_rows = 4 * block
+    quarter = 4 * block
+    half = 8 * block
+    mine = got is not None
+
+    def tile_of(step, info_ref):
+        core = info_ref[CORE]
+        side = core if mine else 1 - core
+        return 4 * (step // 2) + 2 * side + step % 2
+
+    def body(info_ref, left_ref, right_ref, *refs):
+        step = pl.program_id(0)
+        unit = step // 2
+        number = order_number(info_ref, orders, unit)
+        product = turned_times(left_ref[...], right_ref[...])
+        spots = [((4 * (step % 2) + i) ^ number) & 7 for i in range(4)]
+        if not mine:
+            (out_ref,) = refs
+            low = product.astype(LOW)
+            for i, spot in enumerate(spots):
+                row = pl.multiple_of(unit * half + spot * block, block)
+                out_ref[pl.ds(row, block), :] = low[i * block : (i + 1) * block, :]
+            return
+        got_ref, upper_refs, lower_ref = refs[0], refs[1:-1], refs[-1]
+        upper = (step % 2) ^ ((number // 4) % 2)
+        low = []
+        for i, spot in enumerate(spots):
+            row = pl.multiple_of(unit * half + spot * block, block)
+            total = product[i * block : (i + 1) * block, :] + got_ref[pl.ds(row, block), :].astype(FULL)
+            low.append(total.astype(LOW))
+
+        @pl.when(upper == 0)
+        def _():
+            for i, spot in enumerate(spots):
+                row = pl.multiple_of(unit * quarter + (spot & 3) * block, block)
+                lower_ref[pl.ds(row, block), :] = low[i]
+
+        for k in range(units):
+
+            @pl.when((upper == 1) & (unit == k))
+            def _(k=k):
+                for i, spot in enumerate(spots):
+                    row = pl.multiple_of((spot & 3) * block, block)
+                    upper_refs[k][pl.ds(row, block), :] = low[i]
+
+    rows = left.shape[0]
+    operands = [left, right]
+    in_specs = [
+        pl.BlockSpec((rows, tile_rows), lambda s, p: (0, left_of(tile_of(s, p)))),
+        pl.BlockSpec((rows, WIDTH), lambda s, p: (0, right_of(tile_of(s, p)))),
+    ]
+
+    def whole(count):
+        return pl.BlockSpec((count, WIDTH), lambda s, p: (0, 0))
+
+    if mine:
+        operands.append(got)
+        in_specs.append(
+            pl.BlockSpec((units * half, WIDTH), lambda s, p: (0, 0), pipeline_mode=ONE)
+        )
+        counts = [quarter] * units + [units * quarter]
+    else:
+        counts = [units * half]
+    found = pl.pallas_call(
+        body,
+        grid_spec=pltpu.PrefetchScalarGridSpec(
+            num_scalar_prefetch=1,
+            grid=(2 * units,),
+            in_specs=in_specs,
+            out_specs=[whole(c) for c in counts],
+        ),
+        out_shape=[jax.ShapeDtypeStruct((c, WIDTH), LOW) for c in counts],
+        compiler_params=kernel_params(),
+        cost_estimate=pl.CostEstimate(
+            flops=rows * GRAD_ROWS * WIDTH, bytes_accessed=6000000, transcendentals=0
+        ),
+        name="weight_keep" if mine else "weight_send",
+    )(info, *operands)
+    return found if mine else found[0]
+
+
+def widen_out(near, far, info, orders, first_tile, tile_count, columns):
+    units = len(orders)
+    block = GRAD_ROWS // units // 16
+    tall = 4 * block * tile_count // columns
+    pieces = 4 if columns == 1 else 1
+    stride = tall // block
+    first_block = 4 * first_tile
+
+    def body(info_ref, near_ref, far_ref, out_ref):
+        step = pl.program_id(0)
+        for column in range(columns):
+            for piece in range(pieces):
+                index = first_block + column * stride + step * pieces + piece
+                unit = index // 16
+                number = order_number(info_ref, orders, unit)
+                own = (index % 16) // 8 == info_ref[CORE]
+                row = pl.multiple_of((unit * 8 + ((index ^ number) & 7)) * block, block)
+                target = (
+                    slice(piece * block, (piece + 1) * block),
+                    slice(column * WIDTH, (column + 1) * WIDTH),
+                )
+
+                @pl.when(own)
+                def _(row=row, target=target):
+                    out_ref[target] = near_ref[pl.ds(row, block), :].astype(FULL)
+
+                @pl.when(jnp.logical_not(own))
+                def _(row=row, target=target):
+                    out_ref[target] = far_ref[pl.ds(row, block), :].astype(FULL)
+
+    whole = pl.BlockSpec(near.shape, lambda t, p: (0, 0), pipeline_mode=ONE)
+    return pl.pallas_call(
+        body,
+        grid_spec=pltpu.PrefetchScalarGridSpec(
+            num_scalar_prefetch=1,
+            grid=(tall // (pieces * block),),
+            in_specs=[whole, whole],
+            out_specs=pl.BlockSpec((pieces * block, columns * WIDTH), lambda t, p: (t, 0)),
+        ),
+        out_shape=jax.ShapeDtypeStruct((tall, columns * WIDTH), FULL),
+        compiler_params=kernel_params(),
+        cost_estimate=pl.CostEstimate(
+            flops=0, bytes_accessed=tall * columns * WIDTH * 6, transcendentals=0
+        ),
+        name="widen_out",
+    )(info, near, far)
+
+
+def combine(outputs):
+    arrays = []
+
+    def number(array):
+        for k, known in enumerate(arrays):
+            if known is array:
+                return k
+        arrays.append(array)
+        return len(arrays) - 1
+
+    plan = [
+        [[(number(array), row, rows) for array, row, rows in piece] for piece in pieces]
+        for pieces in outputs
+    ]
+    heights = [sum(piece[0][2] for piece in pieces) for pieces in outputs]
+    width = arrays[0].shape[1]
+
+    def body(*refs):
+        sources, targets = refs[: len(arrays)], refs[len(arrays) :]
+        for pieces, target in zip(plan, targets):
+            place = 0
+            for piece in pieces:
+                rows = piece[0][2]
+                for first in range(0, rows, 128):
+                    count = min(128, rows - first)
+                    values = [sources[k][row + first : row + first + count, :] for k, row, _ in piece]
+                    total = values[0] if len(values) == 1 else values[0] + values[1]
+                    target[place + first : place + first + count, :] = total
+                place += rows
+
+    vmem = pl.BlockSpec(memory_space=pltpu.VMEM)
+    return pl.pallas_call(
+        body,
+        in_specs=[vmem] * len(arrays),
+        out_specs=[vmem] * len(outputs),
+        out_shape=[jax.ShapeDtypeStruct((h, width), LOW) for h in heights],
+        compiler_params=kernel_params(),
+        cost_estimate=pl.CostEstimate(
+            flops=0, bytes_accessed=4 * sum(heights) * width, transcendentals=0
+        ),
+        name="combine",
+    )(*arrays)
+
+
+def flow(orders, uppers, lower):
+    units = len(orders)
+    size = lower.shape[0] // units
+    mine = [(lower, k * size, size) for k in range(units)]
+
+    def cut(view, part):
+        array, row, rows = view
+        return array, row + part * rows // 2, rows // 2
+
+    got = yield [(order[0], value) for order, value in zip(orders, uppers)]
+    for level in (1, 2):
+        views = [(g, 0, size) for g in got]
+        away = [[(cut(m, 1), cut(v, 1))] for m, v in zip(mine, views)]
+        kept = [(cut(m, 0), cut(v, 0)) for m, v in zip(mine, views)]
+        size = size // 2
+        *sends, rest = combine(away + [kept])
+        mine = [(rest, k * size, size) for k in range(units)]
+        places = [order[level] for order in orders]
+        got = yield list(zip(places, sends))
+    (joined,) = combine([[(m, (g, 0, size)) for m, g in zip(mine, got)]])
+    (other,) = yield [("w", joined)]
+    values = combine([[((joined, k * size, size), (other, k * size, size))] for k in range(units)])
+    for level in (2, 1, 0):
+        got = yield [(order[level], value) for order, value in zip(orders, values)]
+        pieces = [[((v, 0, size),), ((g, 0, size),)] for v, g in zip(values, got)]
+        size = 2 * size
+        if level > 0:
+            values = combine(pieces)
+    (near,) = combine([sum(pieces, [])])
+    (far,) = yield [("c", near)]
+    return near, far
+
+
+SMALL_SUMS = 96
+SMALL_ROWS = 16
+
+
+def small_flow(packed):
+    for place in "wzyxc":
+        (other,) = yield [(place, packed)]
+        count = packed.shape[0]
+        (packed,) = combine(
+            [
+                [
+                    ((packed, 0, SMALL_SUMS), (other, 0, SMALL_SUMS)),
+                    ((packed, SMALL_SUMS, count - SMALL_SUMS),),
+                    ((other, SMALL_SUMS, count - SMALL_SUMS),),
+                ]
+            ]
+        )
+    return packed
+
+
+def pack_small(sums_zero, sums_one, sums_two, expand_bias, time_total, time_code):
+    pair, code_width = time_code.shape
+    width = sums_one.shape[1]
+    blocks = width // 128
+
+    def body(zero_ref, one_ref, two_ref, bias_ref, total_ref, code_ref, out_ref):
+        bias = [bias_ref[:, k * width : (k + 1) * width] for k in range(4)]
+        rows = jnp.concatenate(
+            [zero_ref[0] + zero_ref[1], one_ref[:3, :], two_ref[:3, :]]
+            + bias
+            + [jnp.zeros((4, width), FULL)],
+            axis=0,
+        ).astype(LOW)
+        for j in range(blocks):
+            out_ref[16 * j : 16 * j + 16, :] = rows[:, 128 * j : 128 * j + 128]
+        totals = [
+            total_ref[s, :, 128 * j : 128 * j + 128] for s in range(pair) for j in range(blocks)
+        ]
+        codes = code_ref[...].astype(FULL)
+        out_ref[SMALL_SUMS:, :] = jnp.concatenate(
+            totals + [codes, jnp.zeros((16 - pair * (blocks + 1), 128), FULL)], axis=0
+        ).astype(LOW)
+
+    return pl.pallas_call(
+        body,
+        out_shape=jax.ShapeDtypeStruct((SMALL_SUMS + SMALL_ROWS, 128), LOW),
+        compiler_params=kernel_params(),
+        name="pack_small",
+    )(sums_zero, sums_one, sums_two, expand_bias, time_total, time_code)
+
+
+def unpack_small(packed, pair, width, code_width):
+    blocks = width // 128
+    count = packed.shape[0]
+    devices = (count - SMALL_SUMS) // SMALL_ROWS
+
+    def body(packed_ref, sums_ref, weight_ref, bias_ref, wide_ref):
+        wide_ref[...] = packed_ref[...].astype(FULL)
+
+        def every(row):
+            return wide_ref[pl.ds(SMALL_SUMS + row, devices, stride=SMALL_ROWS), :]
+
+        codes = [every(pair * blocks + s).astype(LOW) for s in range(pair)]
+        for j in range(blocks):
+            columns = slice(128 * j, 128 * j + 128)
+            sums_ref[:, columns] = wide_ref[16 * j : 16 * j + 16, :]
+            totals = [every(s * blocks + j) for s in range(pair)]
+            weight_ref[:, columns] = sum(
+                turned_times(c, t.astype(LOW)) for c, t in zip(codes, totals)
+            )
+            bias_ref[:, columns] = jnp.sum(sum(totals), axis=0, keepdims=True)
+
+    return pl.pallas_call(
+        body,
+        out_shape=[
+            jax.ShapeDtypeStruct((16, width), FULL),
+            jax.ShapeDtypeStruct((code_width, width), FULL),
+            jax.ShapeDtypeStruct((1, width), FULL),
+        ],
+        scratch_shapes=[pltpu.VMEM((count, 128), FULL)],
+        compiler_params=kernel_params(),
+        name="unpack_small",
+    )(packed)
+
+
+class Order:
+    def __init__(self):
+        self.token = None
+        self.flows = {}
+
+    def after(self, *values):
+        if self.token is None:
+            return values
+        return lax.optimization_barrier((self.token,) + tuple(values))[1:]
+
+    def run(self, function, *values, token=0):
+        found = function(*self.after(*values))
+        self.token = found[token] if isinstance(found, (tuple, list)) else found
+        return found
+
+    def begin(self, name, steps):
+        pairs = next(steps)
+        self.flows[name] = steps, [swap(value, place) for place, value in pairs]
+
+    def advance(self, name):
+        steps, got = self.flows[name]
+        try:
+            pairs = steps.send(list(self.after(*got)))
+        except StopIteration as stop:
+            return stop.value
+        self.token = pairs[0][1]
+        self.flows[name] = steps, [swap(value, place) for place, value in pairs]
+        return None
+
+
+VMEM_LIMIT = 21 * 1024 * 1024
+ONE = pl.Buffered(1)
+
+
+def kernel_params():
+    return pltpu.CompilerParams(vmem_limit_bytes=VMEM_LIMIT)
+
+
+def times(left, right):
+    return jnp.dot(left, right, preferred_element_type=FULL)
+
+
+def times_turned(left, right):
+    return lax.dot_general(left, right, (((1,), (1,)), ((), ())), preferred_element_type=FULL)
+
+
+def turned_times(left, right):
+    return lax.dot_general(left, right, (((0,), (0,)), ((), ())), preferred_element_type=FULL)
+
+
+def split_rows(values, info):
+    near, group, width = values.shape
+    pair = group // 2
+    count = near * group
+
+    def body(info_ref, values_ref, away_ref, own_ref):
+        side = info_ref[SIDE]
+        rows = values_ref[...].reshape(count, width)
+        row = lax.broadcasted_iota(jnp.int32, (count, count), 0)
+        column = lax.broadcasted_iota(jnp.int32, (count, count), 1)
+        half = pair * near
+        first = jnp.where(row < half, pair * (1 - side), pair * side)
+        place = jnp.where(row < half, row, row - half)
+        source = (place % near) * group + first + place // near
+        pick = (source == column).astype(FULL).astype(LOW)
+        moved = times(pick, rows).astype(LOW)
+        away_ref[...] = moved[:half].reshape(pair, near, width)
+        own_ref[...] = moved[half:].reshape(pair, near, width)
+
+    shape = jax.ShapeDtypeStruct((pair, near, width), values.dtype)
+    return pl.pallas_call(
+        body,
+        in_specs=[
+            pl.BlockSpec(memory_space=pltpu.SMEM),
+            pl.BlockSpec(memory_space=pltpu.VMEM),
+        ],
+        out_shape=[shape, shape],
+        compiler_params=kernel_params(),
+        name="split_rows",
+    )(info, values)
+
+
+def join_rows(own, got, info):
+    pair, near, width = own.shape
+    group = 2 * pair
+    count = near * group
+
+    def body(info_ref, own_ref, got_ref, out_ref):
+        side = info_ref[SIDE]
+        row = lax.broadcasted_iota(jnp.int32, (count, count), 0)
+        column = lax.broadcasted_iota(jnp.int32, (count, count), 1)
+        half = pair * near
+        sequence = row % group
+        position = row // group
+        from_own = sequence // pair == side
+        source = jnp.where(from_own, 0, half) + (sequence % pair) * near + position
+        pick = (source == column).astype(FULL).astype(LOW)
+        rows = jnp.concatenate(
+            [own_ref[...].reshape(half, width), got_ref[...].reshape(half, width)], axis=0
+        )
+        out_ref[...] = times(pick, rows).astype(LOW).reshape(near, group, width)
+
+    return pl.pallas_call(
+        body,
+        in_specs=[
+            pl.BlockSpec(memory_space=pltpu.SMEM),
+            pl.BlockSpec(memory_space=pltpu.VMEM),
+            pl.BlockSpec(memory_space=pltpu.VMEM),
+        ],
+        out_shape=jax.ShapeDtypeStruct((near, group, width), own.dtype),
+        compiler_params=kernel_params(),
+        name="join_rows",
+    )(info, own, got)
+
+
+QUERY_BIAS, VALUE_BIAS, OUTPUT_BIAS, FIRST_GAIN, FIRST_SHIFT = range(5)
+NARROW_BIAS, SECOND_GAIN, SECOND_SHIFT = range(5, 8)
+
+
+def head_masks(scale):
+    lane = lax.broadcasted_iota(jnp.int32, (1, 2 * HEAD), 1)
+    first = jnp.where(lane < HEAD, scale, 0.0).astype(LOW)
+    second = jnp.where(lane < HEAD, 0.0, scale).astype(LOW)
+    return first, second
+
+
+def attend(own, got, embed, mixing_weight, output_weight, vectors):
+    pair, near, width = own.shape
+    length = 2 * near
+    scale = 1.0 / math.sqrt(HEAD)
+    duo = 2 * HEAD
+
+    def body(own_ref, got_ref, embed_ref, mix_ref, wout_ref, vec_ref, left_ref, packed_ref,
+             probs_ref, centred_ref, scale_ref, norm_ref):
+        hidden = jnp.concatenate([own_ref[0], got_ref[0]], axis=0).astype(FULL) + embed_ref[0]
+        hidden_low = hidden.astype(LOW)
+        left_ref[:, :width] = hidden_low
+        for part, bias in ((0, QUERY_BIAS), (1, None), (2, VALUE_BIAS)):
+            columns = slice(part * width, (part + 1) * width)
+            product = times(hidden_low, mix_ref[:, columns])
+            if bias is not None:
+                product = product + vec_ref[bias : bias + 1, :]
+            packed_ref[:, columns] = product.astype(LOW)
+        masks = head_masks(scale)
+        lane = lax.broadcasted_iota(jnp.int32, (length, duo), 1)
+        for j in range(width // duo):
+            query = packed_ref[:, j * duo : (j + 1) * duo]
+            key = packed_ref[:, width + j * duo : width + (j + 1) * duo]
+            value = packed_ref[:, 2 * width + j * duo : 2 * width + (j + 1) * duo]
+            found = []
+            for head in range(2):
+                scores = times_turned(query * masks[head], key)
+                peak = jnp.max(scores, axis=-1, keepdims=True)
+                powered = jnp.exp(scores - peak)
+                total = jnp.sum(powered, axis=-1, keepdims=True)
+                low = (powered * (1.0 / total)).astype(LOW)
+                probs_ref[0, 2 * j + head] = low
+                found.append(times(low, value))
+            left_ref[:, width + j * duo : width + (j + 1) * duo] = jnp.where(
+                lane < HEAD, found[0], found[1]
+            ).astype(LOW)
+        first_sum = (
+            hidden
+            + times(left_ref[:, width:], wout_ref[...])
+            + vec_ref[OUTPUT_BIAS : OUTPUT_BIAS + 1, :]
+        )
+        centred = first_sum - jnp.mean(first_sum, axis=-1, keepdims=True)
+        variance = jnp.mean(centred * centred, axis=-1, keepdims=True)
+        inverse = lax.rsqrt(variance + epsilon)
+        centred = centred * inverse
+        centred_ref[...] = centred
+        scale_ref[...] = jnp.broadcast_to(inverse, (length, 128))
+        norm_ref[...] = (
+            centred * vec_ref[FIRST_GAIN : FIRST_GAIN + 1, :]
+            + vec_ref[FIRST_SHIFT : FIRST_SHIFT + 1, :]
+        ).astype(LOW)
+
+    rows = pair * length
+    half = pl.BlockSpec((1, near, width), lambda s: (s, 0, 0))
+
+    def by_rows(columns):
+        return pl.BlockSpec((length, columns), lambda s: (s, 0))
+
+    def whole(array):
+        return pl.BlockSpec(array.shape, lambda s: (0,) * array.ndim, pipeline_mode=ONE)
+
+    return pl.pallas_call(
+        body,
+        grid=(pair,),
+        in_specs=[
+            half,
+            half,
+            pl.BlockSpec((1, 1, width), lambda s: (s, 0, 0)),
+            whole(mixing_weight),
+            whole(output_weight),
+            whole(vectors),
+        ],
+        out_specs=[
+            by_rows(2 * width),
+            by_rows(3 * width),
+            pl.BlockSpec((1, HEADS, length, length), lambda s: (s, 0, 0, 0)),
+            by_rows(width),
+            by_rows(128),
+            by_rows(width),
+        ],
+        out_shape=[
+            jax.ShapeDtypeStruct((rows, 2 * width), LOW),
+            jax.ShapeDtypeStruct((rows, 3 * width), LOW),
+            jax.ShapeDtypeStruct((pair, HEADS, length, length), LOW),
+            jax.ShapeDtypeStruct((rows, width), FULL),
+            jax.ShapeDtypeStruct((rows, 128), FULL),
+            jax.ShapeDtypeStruct((rows, width), LOW),
+        ],
+        compiler_params=kernel_params(),
+        cost_estimate=pl.CostEstimate(
+            flops=2 * rows * width * 4 * width, bytes_accessed=20000000, transcendentals=0
+        ),
+        name="attend",
+    )(own, got, embed, mixing_weight, output_weight, vectors)
+
+
+def gelu_parts(value):
+    size = jnp.abs(value) * math.sqrt(0.5)
+    t = 1.0 / (1.0 + 0.3275911 * size)
+    tail = t * (
+        0.254829592 + t * (-0.284496736 + t * (1.421413741 + t * (-1.453152027 + t * 1.061405429)))
+    )
+    power = jnp.exp(-size * size)
+    tail = 0.5 * tail * power
+    return jnp.where(value < 0, tail, 1.0 - tail), power * (1.0 / math.sqrt(2.0 * math.pi))
+
+
+STRIP = 512
+LONG = 128
+PART = 768
+UNROLL = 1
+
+
+def sum_eights(value):
+    return jnp.sum(value.reshape(-1, 8, value.shape[-1]), axis=0)
+
+
+def feed(norm_low, centred, widen_weight, widen_bias, narrow_weight, vectors, own_cot, got_cot,
+         info, bounds, weights):
+    rows, width = norm_low.shape
+    pair, near, _ = own_cot.shape
+    length = 2 * near
+    inner = widen_weight.shape[1]
+    chunk = width
+    steps = inner // chunk
+
+    def body(info_ref, bound_ref, weight_ref, norm_ref, centred_ref, wide_ref, wbias_ref, narrow_ref, vec_ref,
+             own_ref, got_ref, act_ref, slope_ref, out_own_ref, out_away_ref, grad_ref, low_ref,
+             sums_ref, pre_ref, total_ref):
+        step = pl.program_id(0)
+        pre_ref[...] = times(norm_ref[...], wide_ref[...])
+
+        def strip(i, carry):
+            row = pl.multiple_of(i * STRIP, STRIP)
+            for c in range(0, chunk, PART):
+                value = pre_ref[pl.ds(row, STRIP), c : c + PART] + wbias_ref[:, c : c + PART]
+                below, density = gelu_parts(value)
+                act_ref[pl.ds(row, STRIP), c : c + PART] = (value * below).astype(LOW)
+                slope_ref[pl.ds(row, STRIP), c : c + PART] = (below + value * density).astype(LOW)
+            return carry
+
+        lax.fori_loop(0, rows // STRIP, strip, 0, unroll=UNROLL)
+        product = times(act_ref[...], narrow_ref[...])
+
+        @pl.when(step == 0)
+        def _():
+            total_ref[...] = product
+
+        @pl.when(step > 0)
+        def _():
+            total_ref[...] += product
+
+        @pl.when(step == steps - 1)
+        def _():
+            side = info_ref[SIDE]
+
+            def vector(k):
+                return vec_ref[k : k + 1, :]
+
+            zero = jnp.zeros((8, width), FULL)
+            sums = (zero, zero, zero)
+            for quarter in range(2 * pair):
+                sequence, far = quarter // 2, quarter % 2
+                cot_ref = got_ref if far else own_ref
+                back_ref = out_away_ref if far else out_own_ref
+                bound = bound_ref[pair * side + sequence]
+                weight = weight_ref[pair * side + sequence]
+                start = jnp.where(side == far, 0, near)
+
+                def finish(i, sums, quarter=quarter, sequence=sequence, cot_ref=cot_ref,
+                           back_ref=back_ref, bound=bound, weight=weight, start=start):
+                    inside = pl.multiple_of(i * LONG, LONG)
+                    row = pl.multiple_of(quarter * near + i * LONG, LONG)
+                    first_norm = (
+                        centred_ref[pl.ds(row, LONG), :] * vector(FIRST_GAIN) + vector(FIRST_SHIFT)
+                    )
+                    total = first_norm + total_ref[pl.ds(row, LONG), :] + vector(NARROW_BIAS)
+                    level = total - jnp.mean(total, axis=-1, keepdims=True)
+                    inverse = lax.rsqrt(jnp.mean(level * level, axis=-1, keepdims=True) + epsilon)
+                    level = level * inverse
+                    back_ref[sequence, pl.ds(inside, LONG), :] = (
+                        level * vector(SECOND_GAIN) + vector(SECOND_SHIFT)
+                    ).astype(LOW)
+                    place = start + inside + lax.broadcasted_iota(jnp.int32, (LONG, 1), 0)
+                    factor = jnp.where(place >= bound, weight, 0.0)
+                    upstream = cot_ref[sequence, pl.ds(inside, LONG), :].astype(FULL) * factor
+                    gained = upstream * vector(SECOND_GAIN)
+                    mean = jnp.mean(gained, axis=-1, keepdims=True)
+                    along = jnp.mean(gained * level, axis=-1, keepdims=True)
+                    grad = inverse * (gained - mean - level * along)
+                    grad_ref[pl.ds(row, LONG), :] = grad
+                    low_ref[pl.ds(row, LONG), :] = grad.astype(LOW)
+                    return (
+                        sums[0] + sum_eights(grad),
+                        sums[1] + sum_eights(upstream * level),
+                        sums[2] + sum_eights(upstream),
+                    )
+
+                sums = lax.fori_loop(0, near // LONG, finish, sums)
+            sums_ref[...] = jnp.concatenate(
+                [jnp.sum(v, axis=0, keepdims=True) for v in sums] + [jnp.zeros((5, width), FULL)],
+                axis=0,
+            )
+
+    def whole(array):
+        return pl.BlockSpec(array.shape, lambda s, *_: (0,) * array.ndim, pipeline_mode=ONE)
+
+    def fixed(shape):
+        return pl.BlockSpec(shape, lambda s, *_: (0,) * len(shape))
+
+    by_columns = pl.BlockSpec((rows, chunk), lambda s, *_: (0, s))
+    half = (pair, near, width)
+    return pl.pallas_call(
+        body,
+        grid_spec=pltpu.PrefetchScalarGridSpec(
+            num_scalar_prefetch=3,
+            grid=(steps,),
+            in_specs=[
+                whole(norm_low),
+                whole(centred),
+                pl.BlockSpec((width, chunk), lambda s, *_: (0, s)),
+                pl.BlockSpec((1, chunk), lambda s, *_: (0, s)),
+                pl.BlockSpec((chunk, width), lambda s, *_: (s, 0)),
+                whole(vectors),
+                whole(own_cot),
+                whole(got_cot),
+            ],
+            out_specs=[
+                by_columns,
+                by_columns,
+                fixed(half),
+                fixed(half),
+                fixed((rows, width)),
+                fixed((rows, width)),
+                fixed((8, width)),
+            ],
+            scratch_shapes=[pltpu.VMEM((rows, chunk), FULL), pltpu.VMEM((rows, width), FULL)],
+        ),
+        out_shape=[
+            jax.ShapeDtypeStruct((rows, inner), LOW),
+            jax.ShapeDtypeStruct((rows, inner), LOW),
+            jax.ShapeDtypeStruct(half, LOW),
+            jax.ShapeDtypeStruct(half, LOW),
+            jax.ShapeDtypeStruct((rows, width), FULL),
+            jax.ShapeDtypeStruct((rows, width), LOW),
+            jax.ShapeDtypeStruct((8, width), FULL),
+        ],
+        compiler_params=kernel_params(),
+        cost_estimate=pl.CostEstimate(
+            flops=4 * rows * width * inner, bytes_accessed=20000000, transcendentals=0
+        ),
+        name="feed",
+    )(info, bounds, weights, norm_low, centred, widen_weight, widen_bias, narrow_weight, vectors,
+      own_cot, got_cot)
+
+
+def feed_back(shrink_low, second_grad, slope, centred, inverse, widen_weight, narrow_weight, vectors):
+    rows, width = shrink_low.shape
+    inner = slope.shape[1]
+    chunk = width
+    steps = inner // chunk
+
+    def body(low_ref, grad_ref, slope_ref, centred_ref, inverse_ref, wide_ref, narrow_ref, vec_ref,
+             pre_ref, bias_ref, first_ref, attn_ref, sums_ref, act_ref, total_ref):
+        step = pl.program_id(0)
+        act_ref[...] = times_turned(low_ref[...], narrow_ref[...])
+
+        def strip(i, sums):
+            row = pl.multiple_of(i * STRIP, STRIP)
+            value = act_ref[pl.ds(row, STRIP), :] * slope_ref[pl.ds(row, STRIP), :].astype(FULL)
+            pre_ref[pl.ds(row, STRIP), :] = value.astype(LOW)
+            return sums + sum_eights(value)
+
+        sums = lax.fori_loop(0, rows // STRIP, strip, jnp.zeros((8, chunk), FULL), unroll=UNROLL)
+        bias_ref[...] = jnp.sum(sums, axis=0, keepdims=True)
+        product = times_turned(pre_ref[...], wide_ref[...])
+
+        @pl.when(step == 0)
+        def _():
+            total_ref[...] = product
+
+        @pl.when(step > 0)
+        def _():
+            total_ref[...] += product
+
+        @pl.when(step == steps - 1)
+        def _():
+            gain = vec_ref[FIRST_GAIN : FIRST_GAIN + 1, :]
+
+            def finish(i, sums):
+                row = pl.multiple_of(i * LONG, LONG)
+                upstream = grad_ref[pl.ds(row, LONG), :] + total_ref[pl.ds(row, LONG), :]
+                level = centred_ref[pl.ds(row, LONG), :]
+                gained = upstream * gain
+                mean = jnp.mean(gained, axis=-1, keepdims=True)
+                along = jnp.mean(gained * level, axis=-1, keepdims=True)
+                grad = inverse_ref[pl.ds(row, LONG), :1] * (gained - mean - level * along)
+                first_ref[pl.ds(row, LONG), :] = grad
+                attn_ref[pl.ds(row, LONG), :] = grad.astype(LOW)
+                return (
+                    sums[0] + sum_eights(grad),
+                    sums[1] + sum_eights(upstream * level),
+                    sums[2] + sum_eights(upstream),
+                )
+
+            zero = jnp.zeros((8, width), FULL)
+            sums = lax.fori_loop(0, rows // LONG, finish, (zero, zero, zero))
+            sums_ref[...] = jnp.concatenate(
+                [jnp.sum(v, axis=0, keepdims=True) for v in sums] + [jnp.zeros((5, width), FULL)],
+                axis=0,
+            )
+
+    def whole(array):
+        return pl.BlockSpec(array.shape, lambda s: (0,) * array.ndim, pipeline_mode=ONE)
+
+    def fixed(shape):
+        return pl.BlockSpec(shape, lambda s: (0,) * len(shape))
+
+    by_columns = pl.BlockSpec((rows, chunk), lambda s: (0, s))
+    return pl.pallas_call(
+        body,
+        grid=(steps,),
+        in_specs=[
+            whole(shrink_low),
+            whole(second_grad),
+            by_columns,
+            whole(centred),
+            whole(inverse),
+            pl.BlockSpec((width, chunk), lambda s: (0, s)),
+            pl.BlockSpec((chunk, width), lambda s: (s, 0)),
+            whole(vectors),
+        ],
+        out_specs=[
+            by_columns,
+            pl.BlockSpec((1, chunk), lambda s: (0, s)),
+            fixed((rows, width)),
+            fixed((rows, width)),
+            fixed((8, width)),
+        ],
+        out_shape=[
+            jax.ShapeDtypeStruct((rows, inner), LOW),
+            jax.ShapeDtypeStruct((1, inner), FULL),
+            jax.ShapeDtypeStruct((rows, width), FULL),
+            jax.ShapeDtypeStruct((rows, width), LOW),
+            jax.ShapeDtypeStruct((8, width), FULL),
+        ],
+        scratch_shapes=[pltpu.VMEM((rows, chunk), FULL), pltpu.VMEM((rows, width), FULL)],
+        compiler_params=kernel_params(),
+        cost_estimate=pl.CostEstimate(
+            flops=4 * rows * width * inner, bytes_accessed=20000000, transcendentals=0
+        ),
+        name="feed_back",
+    )(shrink_low, second_grad, slope, centred, inverse, widen_weight, narrow_weight, vectors)
+
+
+def attend_back(attn_low, packed, probs, output_weight):
+    pair, _, length, _ = probs.shape
+    width = attn_low.shape[1]
+    rows = attn_low.shape[0]
+    scale = 1.0 / math.sqrt(HEAD)
+    duo = 2 * HEAD
+
+    def body(attn_ref, packed_ref, probs_ref, wout_ref, right_ref, sums_ref, context_ref):
+        context_ref[...] = times_turned(attn_ref[...], wout_ref[...]).astype(LOW)
+        masks = head_masks(1.0)
+        lane = lax.broadcasted_iota(jnp.int32, (length, duo), 1)
+        for j in range(width // duo):
+            query = packed_ref[:, j * duo : (j + 1) * duo]
+            key = packed_ref[:, width + j * duo : width + (j + 1) * duo]
+            value = packed_ref[:, 2 * width + j * duo : 2 * width + (j + 1) * duo]
+            upstream = context_ref[:, j * duo : (j + 1) * duo]
+            parts = []
+            for head in range(2):
+                low = probs_ref[0, 2 * j + head]
+                probs_full = low.astype(FULL)
+                slope = times_turned(upstream * masks[head], value)
+                dot = jnp.sum(probs_full * slope, axis=-1, keepdims=True)
+                score = (probs_full * (slope - dot)).astype(LOW)
+                parts.append(
+                    (times(score, key), turned_times(score, query), turned_times(low, upstream))
+                )
+            first, second = parts
+            query_grad = jnp.where(lane < HEAD, first[0], second[0]) * scale
+            key_grad = jnp.where(lane < HEAD, first[1], second[1]) * scale
+            value_grad = jnp.where(lane < HEAD, first[2], second[2])
+            right_ref[:, j * duo : (j + 1) * duo] = query_grad.astype(LOW)
+            right_ref[:, width + j * duo : width + (j + 1) * duo] = key_grad.astype(LOW)
+            right_ref[:, 2 * width + j * duo : 2 * width + (j + 1) * duo] = value_grad.astype(LOW)
+            sums_ref[0, 0:1, j * duo : (j + 1) * duo] = jnp.sum(query_grad, axis=0, keepdims=True)
+            sums_ref[0, 1:2, j * duo : (j + 1) * duo] = jnp.sum(value_grad, axis=0, keepdims=True)
+        right_ref[:, 3 * width :] = attn_ref[...]
+
+    def by_rows(columns):
+        return pl.BlockSpec((length, columns), lambda s: (s, 0))
+
+    return pl.pallas_call(
+        body,
+        grid=(pair,),
+        in_specs=[
+            by_rows(width),
+            by_rows(3 * width),
+            pl.BlockSpec((1, HEADS, length, length), lambda s: (s, 0, 0, 0)),
+            pl.BlockSpec(output_weight.shape, lambda s: (0, 0), pipeline_mode=ONE),
+        ],
+        out_specs=[by_rows(4 * width), pl.BlockSpec((1, 2, width), lambda s: (s, 0, 0))],
+        out_shape=[
+            jax.ShapeDtypeStruct((rows, 4 * width), LOW),
+            jax.ShapeDtypeStruct((pair, 2, width), FULL),
+        ],
+        scratch_shapes=[pltpu.VMEM((length, width), LOW)],
+        compiler_params=kernel_params(),
+        cost_estimate=pl.CostEstimate(
+            flops=2 * rows * width * 4 * width, bytes_accessed=10000000, transcendentals=0
+        ),
+        name="attend_back",
+    )(attn_low, packed, probs, output_weight)
+
+
+def hidden_back(right, first_grad, mixing_weight, pair):
+    rows, width = first_grad.shape
+    length = rows // pair
+    near = length // 2
+
+    def body(right_ref, grad_ref, mix_ref, own_ref, away_ref, total_ref):
+        hidden = grad_ref[...] + times_turned(right_ref[...], mix_ref[...])
+        low = hidden.astype(LOW)
+        own_ref[0] = low[:near]
+        away_ref[0] = low[near:]
+        total_ref[0] = jnp.sum(hidden, axis=0, keepdims=True)
+
+    half = pl.BlockSpec((1, near, width), lambda s: (s, 0, 0))
+    return pl.pallas_call(
+        body,
+        grid=(pair,),
+        in_specs=[
+            pl.BlockSpec((length, 3 * width), lambda s: (s, 0)),
+            pl.BlockSpec((length, width), lambda s: (s, 0)),
+            pl.BlockSpec(mixing_weight.shape, lambda s: (0, 0), pipeline_mode=ONE),
+        ],
+        out_specs=[half, half, pl.BlockSpec((1, 1, width), lambda s: (s, 0, 0))],
+        out_shape=[
+            jax.ShapeDtypeStruct((pair, near, width), LOW),
+            jax.ShapeDtypeStruct((pair, near, width), LOW),
+            jax.ShapeDtypeStruct((pair, 1, width), FULL),
+        ],
+        compiler_params=kernel_params(),
+        cost_estimate=pl.CostEstimate(
+            flops=6 * rows * width * width, bytes_accessed=8000000, transcendentals=0
+        ),
+        name="hidden_back",
+    )(right, first_grad, mixing_weight)
+
+
+def pair_shards(
+    tokens,
+    timesteps,
+    boundary,
+    importance,
+    cotangent,
+    time_weight,
+    time_bias,
+    mixing_weight,
+    query_bias,
+    value_bias,
+    output_weight,
+    output_bias,
+    first_gain,
+    first_shift,
+    widen_weight,
+    widen_bias,
+    narrow_weight,
+    narrow_bias,
+    second_gain,
+    second_shift,
+):
+    near, group, width = tokens.shape
+    pair = group // 2
+    side = lax.axis_index("blk")
+    info = device_info()
+
+    away, own = split_rows(tokens, info)
+    got = swap(away, "x")
+    away_cot, own_cot = split_rows(cotangent, info)
+    got_cot = swap(away_cot, "x")
+    vectors = jnp.stack(
+        [
+            query_bias,
+            value_bias,
+            output_bias,
+            first_gain,
+            first_shift,
+            narrow_bias,
+            second_gain,
+            second_shift,
+        ]
+    ).astype(FULL)
+    time_code = sinusoid(
+        lax.dynamic_slice_in_dim(timesteps, side * pair, pair, 0), time_weight.shape[0]
+    ).astype(LOW)
+    embed = jnp.dot(time_code, time_weight, preferred_element_type=FULL) + time_bias.astype(FULL)
+
+    left, packed, probs, centred, inverse, norm_low = attend(
+        own, got, embed[:, None], mixing_weight, output_weight, vectors
+    )
+    (act_low, slope, out_own, out_away, second_grad, shrink_low, sums_two) = feed(
+        norm_low,
+        centred,
+        widen_weight,
+        widen_bias.astype(FULL)[None],
+        narrow_weight,
+        vectors,
+        own_cot,
+        got_cot,
+        info,
+        boundary,
+        importance,
+    )
+    shrink_of = (SHRINK_ORDERS, lambda t: t, lambda t: 0)
+    expand_of = (EXPAND_ORDERS, lambda t: t % 3, lambda t: t // 3)
+    mixing_of = (MIXING_ORDERS, lambda t: t % 3 + 3 * (t // 9), lambda t: t // 3)
+
+    def send_half(left, right, of):
+        return weight_half(left, right, info, *of)
+
+    def keep_half(left, right, got, of):
+        found = weight_half(left, right, info, *of, got=got)
+        return found[:-1], found[-1]
+
+    line = Order()
+    shrink_send = line.run(partial(send_half, of=shrink_of), act_low, shrink_low)
+    shrink_got = swap(shrink_send, "c")
+    out_got = swap(out_away, "x")
+    pre_low, expand_bias, first_grad, attn_low, sums_one = line.run(
+        feed_back, shrink_low, second_grad, slope, centred, inverse, widen_weight, narrow_weight,
+        vectors, token=4
+    )
+    uppers, lower = line.run(
+        partial(keep_half, of=shrink_of), act_low, shrink_low, shrink_got, token=1
+    )
+    line.begin("S", flow(SHRINK_ORDERS, uppers, lower))
+    expand_send = line.run(partial(send_half, of=expand_of), norm_low, pre_low)
+    expand_got = swap(expand_send, "c")
+    right, sums_zero = line.run(attend_back, attn_low, packed, probs, output_weight, token=1)
+    line.advance("S")
+    uppers, lower = line.run(
+        partial(keep_half, of=expand_of), norm_low, pre_low, expand_got, token=1
+    )
+    line.begin("E", flow(EXPAND_ORDERS, uppers, lower))
+    mixing_send = line.run(partial(send_half, of=mixing_of), left, right)
+    mixing_got = swap(mixing_send, "c")
+    line.advance("S")
+    grad_own, grad_away, time_total = line.run(
+        partial(hidden_back, pair=pair), right, first_grad, mixing_weight, token=2
+    )
+    grad_got = swap(grad_away, "x")
+    uppers, lower = line.run(partial(keep_half, of=mixing_of), left, right, mixing_got, token=1)
+    line.begin("M", flow(MIXING_ORDERS, uppers, lower))
+    small = line.run(pack_small, sums_zero, sums_one, sums_two, expand_bias, time_total, time_code)
+    line.begin("R", small_flow(small))
+    results = {}
+    widens = {
+        "S": lambda near, far: widen_out(near, far, info, SHRINK_ORDERS, 0, 8, 1),
+        "E": lambda near, far: widen_out(near, far, info, EXPAND_ORDERS, 0, 12, 4),
+    }
+    for name in SEQUENCE:
+        if name == "o":
+            output = line.run(partial(join_rows, info=info), out_own, out_got)
+        elif name == "u":
+            sums, time_weight_grad, time_bias_grad = line.run(
+                partial(unpack_small, pair=pair, width=width, code_width=time_code.shape[1]),
+                results["R"],
+            )
+        elif name == "i":
+            input_grad = line.run(partial(join_rows, info=info), grad_own, grad_got)
+        elif name in "SEMR":
+            results[name] = line.advance(name)
+        else:
+            name = name.upper()
+            results[name] = line.run(widens[name], *results[name])
+    mixing_near, mixing_far = results["M"]
+    return (
+        output,
+        input_grad,
+        time_weight_grad,
+        time_bias_grad[0],
+        widen_out(mixing_near, mixing_far, info, MIXING_ORDERS, 0, 9, 3),
+        sums[0],
+        sums[1],
+        widen_out(mixing_near, mixing_far, info, MIXING_ORDERS, 9, 3, 1),
+        sums[2],
+        sums[3],
+        sums[4],
+        results["E"],
+        sums[8:12].reshape(-1),
+        results["S"],
+        sums[5],
+        sums[6],
+        sums[7],
+    )
+
+
+SEQUENCE = "ESoMESMRESMiESMRESMRESMsEMREReuM"
+
+
 def solution(mesh):
+    pairs = mesh.shape["blk"] == 2 and mesh.shape["dp"] == 16
     return jax.shard_map(
-        shards,
+        pair_shards if pairs else general_shards,
         mesh=mesh,
         in_specs=(
             P("blk", "dp", None),

time: 772 us -> 270 us (0.35)
  waiting for transfers between devices: 343 us -> 79.1 us
  blocking collectives: 159 us -> 0 us
  matrix products: 107 us -> 0.14 us
  Pallas kernels: 0 us -> 95.3 us
  other arithmetic: 73.9 us -> 2.92 us
  starting transfers between devices: 1.67 us -> 71.8 us
  local copies, waits for them, and re-layouts: 66.2 us -> 18.8 us
  between operations: 17.4 us -> 1.29 us
    reduce_scatter x5 -> x0, waiting for transfers between devices: 241 us -> none  [the longest x1 79.6 us: reduce_dp(): lax.psum_scatter(parts[9].astype(jnp.bfloat16), 'dp', scatter_dimension=0...]
    unnamed x2 -> x0, blocking collectives: 120 us -> none
    dot_general x21 -> x1, matrix products: 107 us -> 0.14 us  [pair_shards(): jnp.dot(time_code, time_weight, preferred_element_type=FULL)]
    pallas_call x0 -> x47, Pallas kernels: none -> 95.3 us  [the longest x6 22.1 us: weight_half(): pl.pallas_call(body, grid_spec=pltpu.PrefetchScalarGridSpec(num_scalar_pr...]
    ppermute x0 -> x66, waiting for transfers between devices: none -> 79.1 us  [swap(): return lax.ppermute(value, axis, [(i, i ^ bit) for i in range(count)])]
    ppermute x0 -> x66, starting transfers between devices: none -> 71.8 us  [swap(): return lax.ppermute(value, axis, [(i, i ^ bit) for i in range(count)])]
    all_gather x7 -> x0, waiting for transfers between devices: 68.2 us -> none  [the longest x1 37.4 us: reduce_dp(): lax.all_gather(summed[11].astype(jnp.bfloat16), 'dp', axis=0, tiled=True)]
    convert_element_type x25 -> x2, other arithmetic: 57.8 us -> 0.69 us  [the longest x1 0.68 us: pair_shards(): time_bias.astype(FULL)]
  transfers between devices with their start and end apart: 13 -> 66, of which waited for: 7 -> 27; matrix products, arithmetic and copies ran while one was open for 30% -> 3% of each run, Pallas kernels for 0% -> 20%
where the time goes in v1:
time: 270 us; the launch traced here: 269 us
  Pallas kernels  95.3 us (35%)
  waiting for transfers between devices  79.1 us (29%)
  starting transfers between devices  71.8 us (27%)
  local copies, waits for them, and re-layouts  18.8 us (7%)
  other arithmetic  2.92 us (1%)
    ppermute x66, waiting for transfers between devices, swap(): return lax.ppermute(value, axis, [(i, i ^ bit) for i in range(count)])  79.1 us
    ppermute x66, starting transfers between devices, swap(): return lax.ppermute(value, axis, [(i, i ^ bit) for i in range(count)])  71.8 us
    pallas_call x6, Pallas kernels, weight_half(): pl.pallas_call(body, grid_spec=pltpu.PrefetchScalarGridSpec(num_scalar_pr...  22.1 us
    pallas_call x4, Pallas kernels, widen_out(): pl.pallas_call(body, grid_spec=pltpu.PrefetchScalarGridSpec(num_scalar_pr...  21.3 us
    pallas_call x1, Pallas kernels, feed(): pl.pallas_call(body, grid_spec=pltpu.PrefetchScalarGridSpec(num_scalar_pr...  14.2 us
    unnamed x32, local copies, waits for them, and re-layouts  11.9 us
    pallas_call x1, Pallas kernels, attend_back(): pl.pallas_call(body, grid=(pair,), in_specs=[by_rows(width), by_rows(3 *...  10.1 us
    pallas_call x1, Pallas kernels, feed_back(): pl.pallas_call(body, grid=(steps,), in_specs=[whole(shrink_low), whole(se...  8.68 us
  transfers between devices with their start and end apart: 66, of which 27 were waited for; matrix products, arithmetic and copies ran while one was open for 3% of the time, Pallas kernels for 20%

profile of v1, /device:TPU:0, one launch (start us, length us, event | category | flops | bytes accessed | tf_op | source)
XLA Modules:
  0.0 269.4 jit_solution(11655270770581219490)
XLA Ops:
  19.8 7.3 %attend.1 = (bf16[512,1536]{1,0:T(8,128)(2,1)S(1)}, bf16[512,2304]{1,0:T(8,128)(2,1)S(1)}, bf16[2,12,256,256]{3,2,1,0:T(8,128)(2,1)S(1)}, f32[512,768]{1,0:T(8,1...) custom-call(bf16[2,128,768]{2,1,0:T(8,128)(2,1)S(1)} %get-tuple-element.206.own_ref, ...), custom_call_target="tpu_custom_call" | custom-call | flops 2415919104 | bytes 20000000 | tf_op jit(solution)/shard_map/attend/pallas_call | solution.py:896
  33.5 14.2 %feed.1 = (bf16[512,3072]{1,0:T(8,128)(2,1)S(1)}, bf16[512,3072]{1,0:T(8,128)(2,1)S(1)}, bf16[2,128,768]{2,1,0:T(8,128)(2,1)S(1)}, bf16[2,128,768]{2,1,0:T(8,128...) custom-call(s32[6]{0:T(128)S(1)} %stack.54.info_ref, s32[4]{0:T(128)S(1)} %copy-done.10, ...), custom_call_target="tpu_custom_call" | custom-call | flops 4831838208 | bytes 20000000 | tf_op jit(solution)/shard_map/feed/pallas_call | solution.py:1047
  50.7 8.7 %feed_back.1 = (bf16[512,3072]{1,0:T(8,128)(2,1)S(1)}, f32[1,3072]{1,0:T(1,128)S(1)}, f32[512,768]{1,0:T(8,128)S(1)}, bf16[512,768]{1,0:T(8,128)(2,1)S(1)}, f32[8,768]{1,0:T(8,128)S(1)}) custom-call(bf16[512,768]{1,0:T(8,128)(2,1)S(1)} %get-tuple-element.227.right_ref.low_ref, f32[512,768]{1,0:T(8,128)S(1)} %get-tuple-element.218.grad_ref, ...), custom_call_target="tpu_custom_call" | custom-call | flops 4831838208 | bytes 20000000 | tf_op jit(solution)/shard_map/feed_back/pallas_call | solution.py:1154
  62.6 3.7 %weight_send.4 = bf16[1536,768]{1,0:T(8,128)(2,1)S(1)} custom-call(s32[6]{0:T(128)S(1)} %stack.54.info_ref, bf16[512,768]{1,0:T(8,128)(2,1)S(1)} %get-tuple-element.247.norm_ref.left_ref, bf16[512,3072]{1,0:T(8,128)(2,1)S(1)} %get-tuple-element.248.right_ref), custom_call_target="tpu_custom_call" | custom-call | flops 1207959552 | bytes 6000000 | tf_op jit(solution)/shard_map/weight_send/pallas_call | solution.py:482
  70.4 10.1 %attend_back.1 = (bf16[512,3072]{1,0:T(8,128)(2,1)S(1)}, f32[2,2,768]{2,1,0:T(2,128)S(1)}) custom-call(bf16[512,768]{1,0:T(8,128)(2,1)S(1)} %get-tuple-element.236.attn_ref, bf16[512,2304]{1,0:T(8,128)(2,1)S(1)} %get-tuple-element.237.packed_ref, bf16[2,12,256,256]{3,2,1,0:T(8,128)(2,1)S(1)} %copy-done.13, bf16[768,768]{1,0:T(8,128)(2,1)S(1)} %copy-done.9), custom_call_target="tpu_custom_call" | custom-call | flops 2415919104 | bytes 10000000 | tf_op jit(solution)/shard_map/attend_back/pallas_call | solution.py:1230
  84.1 4.0 %weight_keep.4 = (bf16[256,768]{1,0:T(8,128)(2,1)S(1)}, bf16[256,768]{1,0:T(8,128)(2,1)S(1)}, bf16[256,768]{1,0:T(8,128)(2,1)S(1)}, bf16[768,768]{1,0:T(8,128)(2,1)S(1)}) custom-call(s32[6]{0:T(128)S(1)} %stack.54.info_ref, bf16[512,768]{1,0:T(8,128)(2,1)S(1)} %get-tuple-element.247.norm_ref.left_ref, bf16[512,3072]{1,0:T(8,128)(2,1)S(1)} %get-tuple-element.248.right_ref, ...), custom_call_target="tpu_custom_call" | custom-call | flops 1207959552 | bytes 6000000 | tf_op jit(solution)/shard_map/weight_keep/pallas_call | solution.py:482
  88.2 3.9 %weight_send.5 = bf16[1536,768]{1,0:T(8,128)(2,1)S(1)} custom-call(s32[6]{0:T(128)S(1)} %stack.54.info_ref, bf16[512,1536]{1,0:T(8,128)(2,1)S(1)} %get-tuple-element.265.left_ref, bf16[512,3072]{1,0:T(8,128)(2,1)S(1)} %get-tuple-element.266.right_ref), custom_call_target="tpu_custom_call" | custom-call | flops 1207959552 | bytes 6000000 | tf_op jit(solution)/shard_map/weight_send/pallas_call | solution.py:482
  96.3 5.7 %collective-permute-done.7.refs_2_ = bf16[192,768]{1,0:T(8,128)(2,1)S(1)} collective-permute-done((bf16[192,768]{1,0:T(8,128)(2,1)S(1)}, bf16[192,768]{1,0:T(8,128)(2,1)S(1)}, u32[]{:S(2)}, u32[]{:S(2)}) %collective-permute-start.7) | collective-permute-done | bytes 294944 | tf_op jit(solution)/shard_map/ppermute | solution.py:390
  107.7 4.3 %weight_keep.5 = (bf16[256,768]{1,0:T(8,128)(2,1)S(1)}, bf16[256,768]{1,0:T(8,128)(2,1)S(1)}, bf16[256,768]{1,0:T(8,128)(2,1)S(1)}, bf16[768,768]{1,0:T(8,128)(2,1)S(1)}) custom-call(s32[6]{0:T(128)S(1)} %stack.54.info_ref, bf16[512,1536]{1,0:T(8,128)(2,1)S(1)} %get-tuple-element.265.left_ref, bf16[512,3072]{1,0:T(8,128)(2,1)S(1)} %get-tuple-element.266.right_ref, ...), custom_call_target="tpu_custom_call" | custom-call | flops 1207959552 | bytes 6000000 | tf_op jit(solution)/shard_map/weight_keep/pallas_call | solution.py:482
  113.4 5.4 %collective-permute-done.9.refs_1_ = bf16[256,768]{1,0:T(8,128)(2,1)S(1)} collective-permute-done((bf16[256,768]{1,0:T(8,128)(2,1)S(1)}, bf16[256,768]{1,0:T(8,128)(2,1)S(1)}, u32[]{:S(2)}, u32[]{:S(2)}) %collective-permute-start.9) | collective-permute-done | bytes 393248 | tf_op jit(solution)/shard_map/ppermute | solution.py:390
  122.6 11.5 %collective-permute-done.13.refs_2_ = bf16[96,768]{1,0:T(8,128)(2,1)S(1)} collective-permute-done((bf16[96,768]{1,0:T(8,128)(2,1)S(1)}, bf16[96,768]{1,0:T(8,128)(2,1)S(1)}, u32[]{:S(2)}, u32[]{:S(2)}) %collective-permute-start.13) | collective-permute-done | bytes 147488 | tf_op jit(solution)/shard_map/ppermute | solution.py:390
  151.0 4.5 %collective-permute-done.25.refs_1_ = bf16[112,128]{1,0:T(8,128)(2,1)S(1)} collective-permute-done((bf16[112,128]{1,0:T(8,128)(2,1)S(1)}, bf16[112,128]{1,0:T(8,128)(2,1)S(1)}, u32[]{:S(2)}, u32[]{:S(2)}) %collective-permute-start.25) | collective-permute-done | bytes 28704 | tf_op jit(solution)/shard_map/ppermute | solution.py:390
  172.7 4.3 %collective-permute-done.33.refs_3_ = bf16[64,768]{1,0:T(8,128)(2,1)S(1)} collective-permute-done((bf16[64,768]{1,0:T(8,128)(2,1)S(1)}, bf16[64,768]{1,0:T(8,128)(2,1)S(1)}, u32[]{:S(2)}, u32[]{:S(2)}) %collective-permute-start.33) | collective-permute-done | bytes 98336 | tf_op jit(solution)/shard_map/ppermute | solution.py:390
  177.8 3.9 %collective-permute-done.31.refs_1_ = bf16[64,768]{1,0:T(8,128)(2,1)S(1)} collective-permute-done((bf16[64,768]{1,0:T(8,128)(2,1)S(1)}, bf16[64,768]{1,0:T(8,128)(2,1)S(1)}, u32[]{:S(2)}, u32[]{:S(2)}) %collective-permute-start.31) | collective-permute-done | bytes 98336 | tf_op jit(solution)/shard_map/ppermute | solution.py:390
  186.0 3.7 %collective-permute-start.38 = (bf16[192,768]{1,0:T(8,128)(2,1)S(1)}, bf16[192,768]{1,0:T(8,128)(2,1)S(1)}, u32[]{:S(2)}, u32[]{:S(2)}) collective-permute-start(bf16[192,768]{1,0:T(8,128)(2,1)S(1)} %combine.37.refs_0_), channel_id=1, source_target_pairs={{0,16},{2,18},{4,20},{6,22},{8,24},{10,26},{12,28},{14,30},{16,0},... | collective-permute-start | bytes 884744 | tf_op jit(solution)/shard_map/ppermute | solution.py:390
  191.5 3.9 %collective-permute-done.39.refs_1_ = bf16[128,128]{1,0:T(8,128)(2,1)S(1)} collective-permute-done((bf16[128,128]{1,0:T(8,128)(2,1)S(1)}, bf16[128,128]{1,0:T(8,128)(2,1)S(1)}, u32[]{:S(2)}, u32[]{:S(2)}) %collective-permute-start.39) | collective-permute-done | bytes 32800 | tf_op jit(solution)/shard_map/ppermute | solution.py:390
  210.8 3.4 %collective-permute-done.45.refs_1_ = bf16[64,768]{1,0:T(8,128)(2,1)S(1)} collective-permute-done((bf16[64,768]{1,0:T(8,128)(2,1)S(1)}, bf16[64,768]{1,0:T(8,128)(2,1)S(1)}, u32[]{:S(2)}, u32[]{:S(2)}) %collective-permute-start.45) | collective-permute-done | bytes 98336 | tf_op jit(solution)/shard_map/ppermute | solution.py:390
  214.8 3.7 %collective-permute-done.48.refs_1_ = bf16[160,128]{1,0:T(8,128)(2,1)S(1)} collective-permute-done((bf16[160,128]{1,0:T(8,128)(2,1)S(1)}, bf16[160,128]{1,0:T(8,128)(2,1)S(1)}, u32[]{:S(2)}, u32[]{:S(2)}) %collective-permute-start.48) | collective-permute-done | bytes 40992 | tf_op jit(solution)/shard_map/ppermute | solution.py:390
  222.2 4.0 %collective-permute-done.53.refs_3_ = bf16[128,768]{1,0:T(8,128)(2,1)S(1)} collective-permute-done((bf16[128,768]{1,0:T(8,128)(2,1)S(1)}, bf16[128,768]{1,0:T(8,128)(2,1)S(1)}, u32[]{:S(2)}, u32[]{:S(2)}) %collective-permute-start.53) | collective-permute-done | bytes 196640 | tf_op jit(solution)/shard_map/ppermute | solution.py:390
  228.7 3.3 %collective-permute-done.52.refs_1_ = bf16[128,768]{1,0:T(8,128)(2,1)S(1)} collective-permute-done((bf16[128,768]{1,0:T(8,128)(2,1)S(1)}, bf16[128,768]{1,0:T(8,128)(2,1)S(1)}, u32[]{:S(2)}, u32[]{:S(2)}) %collective-permute-start.52) | collective-permute-done | bytes 196640 | tf_op jit(solution)/shard_map/ppermute | solution.py:390
  234.8 5.6 %widen_out.4 = f32[3072,768]{1,0:T(8,128)} custom-call(s32[6]{0:T(128)S(1)} %stack.54.info_ref, bf16[1536,768]{1,0:T(8,128)(2,1)S(1)} %combine.43.near_ref, bf16[1536,768]{1,0:T(8,128)(2,1)S(1)} %collective-permute-done.55.far_ref), custom_call_target="tpu_custom_call" | custom-call | bytes 14155776 | tf_op jit(solution)/shard_map/widen_out/pallas_call | solution.py:531
  245.3 4.1 %collective-permute-done.62.refs_1_ = bf16[224,128]{1,0:T(8,128)(2,1)S(1)} collective-permute-done((bf16[224,128]{1,0:T(8,128)(2,1)S(1)}, bf16[224,128]{1,0:T(8,128)(2,1)S(1)}, u32[]{:S(2)}, u32[]{:S(2)}) %collective-permute-start.62) | collective-permute-done | bytes 57376 | tf_op jit(solution)/shard_map/ppermute | solution.py:390
  250.8 6.9 %widen_out.5 = f32[768,3072]{1,0:T(8,128)} custom-call(s32[6]{0:T(128)S(1)} %stack.54.info_ref, bf16[1536,768]{1,0:T(8,128)(2,1)S(1)} %combine.48.near_ref, bf16[1536,768]{1,0:T(8,128)(2,1)S(1)} %collective-permute-done.63.far_ref), custom_call_target="tpu_custom_call" | custom-call | bytes 14155776 | tf_op jit(solution)/shard_map/widen_out/pallas_call | solution.py:531
  262.0 6.2 %widen_out.6 = f32[768,2304]{1,0:T(8,128)} custom-call(s32[6]{0:T(128)S(1)} %stack.54.info_ref, bf16[1536,768]{1,0:T(8,128)(2,1)S(1)} %combine.49.near_ref, bf16[1536,768]{1,0:T(8,128)(2,1)S(1)} %collective-permute-done.65.far_ref), custom_call_target="tpu_custom_call" | custom-call | bytes 10616832 | tf_op jit(solution)/shard_map/widen_out/pallas_call | solution.py:531
  (211 shorter events, 131.5 us)
Async XLA Ops:
  8.4 20.4 %collective-permute-start.1 = (bf16[2,128,768]{2,1,0:T(8,128)(2,1)S(1)}, bf16[2,128,768]{2,1,0:T(8,128)(2,1)S(1)}, u32[]{:S(2)}, u32[]{:S(2)}) collective-permute-start(bf16[2,128,768]{2,1,0:T(8,128)(2,1)S(1)} %get-tuple-element.211), channel_id=1, source_target_pairs={{0,1},{1,0},{2,3},{3,2},{4,5},{5,4},{6,7},{7,6},{8,9},{9,8},{10,11... | collective-permute-start | bytes 1179656 | tf_op jit(solution)/shard_map/ppermute | solution.py:390
  66.4 17.7 %collective-permute-start.5 = (bf16[1536,768]{1,0:T(8,128)(2,1)S(1)}, bf16[1536,768]{1,0:T(8,128)(2,1)S(1)}, u32[]{:S(2)}, u32[]{:S(2)}) collective-permute-start(bf16[1536,768]{1,0:T(8,128)(2,1)S(1)} %weight_send.4), channel_id=1, source_target_pairs={{0,2},{2,0},{4,6},{6,4},{8,10},{10,8},{12,14},{14,12},{16,18},{18,... | collective-permute-start | bytes 7077896 | tf_op jit(solution)/shard_map/ppermute | solution.py:390
  66.9 15.6 %collective-permute-start.3 = (bf16[384,768]{1,0:T(8,128)(2,1)S(1)}, bf16[384,768]{1,0:T(8,128)(2,1)S(1)}, u32[]{:S(2)}, u32[]{:S(2)}) collective-permute-start(bf16[384,768]{1,0:T(8,128)(2,1)S(1)} %get-tuple-element.241), channel_id=1, source_target_pairs={{0,1},{1,0},{2,3},{3,2},{4,5},{5,4},{6,7},{7,6},{8,9},{9,8},{10,11... | collective-permute-start | bytes 1769480 | tf_op jit(solution)/shard_map/ppermute | solution.py:390
  68.9 15.0 %collective-permute-start.4 = (bf16[384,768]{1,0:T(8,128)(2,1)S(1)}, bf16[384,768]{1,0:T(8,128)(2,1)S(1)}, u32[]{:S(2)}, u32[]{:S(2)}) collective-permute-start(bf16[384,768]{1,0:T(8,128)(2,1)S(1)} %get-tuple-element.242), channel_id=1, source_target_pairs={{0,4},{2,6},{4,0},{6,2},{8,12},{10,14},{12,8},{14,10},{16,20},{18,... | collective-permute-start | bytes 1769480 | tf_op jit(solution)/shard_map/ppermute | solution.py:390
  92.1 15.7 %collective-permute-start.8 = (bf16[1536,768]{1,0:T(8,128)(2,1)S(1)}, bf16[1536,768]{1,0:T(8,128)(2,1)S(1)}, u32[]{:S(2)}, u32[]{:S(2)}) collective-permute-start(bf16[1536,768]{1,0:T(8,128)(2,1)S(1)} %weight_send.5), channel_id=1, source_target_pairs={{0,2},{2,0},{4,6},{6,4},{8,10},{10,8},{12,14},{14,12},{16,18},{18,... | collective-permute-start | bytes 7077896 | tf_op jit(solution)/shard_map/ppermute | solution.py:390
  94.3 18.4 %collective-permute-start.14 = (bf16[2,128,768]{2,1,0:T(8,128)(2,1)S(1)}, bf16[2,128,768]{2,1,0:T(8,128)(2,1)S(1)}, u32[]{:S(2)}, u32[]{:S(2)}) collective-permute-start(bf16[2,128,768]{2,1,0:T(8,128)(2,1)S(1)} %get-tuple-element.288), channel_id=1, source_target_pairs={{0,1},{1,0},{2,3},{3,2},{4,5},{5,4},{6,7},{7,6},{8,9},{9,8},{10,11... | collective-permute-start | bytes 1179656 | tf_op jit(solution)/shard_map/ppermute | solution.py:390
  95.7 23.1 %collective-permute-start.9 = (bf16[256,768]{1,0:T(8,128)(2,1)S(1)}, bf16[256,768]{1,0:T(8,128)(2,1)S(1)}, u32[]{:S(2)}, u32[]{:S(2)}) collective-permute-start(bf16[256,768]{1,0:T(8,128)(2,1)S(1)} %get-tuple-element.277), channel_id=1, source_target_pairs={{0,1},{1,0},{2,3},{3,2},{4,5},{5,4},{6,7},{7,6},{8,9},{9,8},{10,11... | collective-permute-start | bytes 1179656 | tf_op jit(solution)/shard_map/ppermute | solution.py:390
  102.0 18.4 %collective-permute-start.10 = (bf16[256,768]{1,0:T(8,128)(2,1)S(1)}, bf16[256,768]{1,0:T(8,128)(2,1)S(1)}, u32[]{:S(2)}, u32[]{:S(2)}) collective-permute-start(bf16[256,768]{1,0:T(8,128)(2,1)S(1)} %get-tuple-element.278), channel_id=1, source_target_pairs={{0,4},{2,6},{4,0},{6,2},{8,12},{10,14},{12,8},{14,10},{16,20},{18,... | collective-permute-start | bytes 1179656 | tf_op jit(solution)/shard_map/ppermute | solution.py:390
  103.5 17.4 %collective-permute-start.11 = (bf16[256,768]{1,0:T(8,128)(2,1)S(1)}, bf16[256,768]{1,0:T(8,128)(2,1)S(1)}, u32[]{:S(2)}, u32[]{:S(2)}) collective-permute-start(bf16[256,768]{1,0:T(8,128)(2,1)S(1)} %get-tuple-element.279), channel_id=1, source_target_pairs={{0,8},{2,10},{4,12},{6,14},{8,0},{10,2},{12,4},{14,6},{16,24},{18,... | collective-permute-start | bytes 1179656 | tf_op jit(solution)/shard_map/ppermute | solution.py:390
  112.1 25.6 %collective-permute-start.15 = (bf16[256,768]{1,0:T(8,128)(2,1)S(1)}, bf16[256,768]{1,0:T(8,128)(2,1)S(1)}, u32[]{:S(2)}, u32[]{:S(2)}) collective-permute-start(bf16[256,768]{1,0:T(8,128)(2,1)S(1)} %get-tuple-element.291), channel_id=1, source_target_pairs={{0,1},{1,0},{2,3},{3,2},{4,5},{5,4},{6,7},{7,6},{8,9},{9,8},{10,11... | collective-permute-start | bytes 1179656 | tf_op jit(solution)/shard_map/ppermute | solution.py:390
  112.7 27.8 %collective-permute-start.16 = (bf16[256,768]{1,0:T(8,128)(2,1)S(1)}, bf16[256,768]{1,0:T(8,128)(2,1)S(1)}, u32[]{:S(2)}, u32[]{:S(2)}) collective-permute-start(bf16[256,768]{1,0:T(8,128)(2,1)S(1)} %get-tuple-element.292), channel_id=1, source_target_pairs={{0,4},{2,6},{4,0},{6,2},{8,12},{10,14},{12,8},{14,10},{16,20},{18,... | collective-permute-start | bytes 1179656 | tf_op jit(solution)/shard_map/ppermute | solution.py:390
  118.9 25.2 %collective-permute-start.17 = (bf16[256,768]{1,0:T(8,128)(2,1)S(1)}, bf16[256,768]{1,0:T(8,128)(2,1)S(1)}, u32[]{:S(2)}, u32[]{:S(2)}) collective-permute-start(bf16[256,768]{1,0:T(8,128)(2,1)S(1)} %get-tuple-element.293), channel_id=1, source_target_pairs={{0,8},{2,10},{4,12},{6,14},{8,0},{10,2},{12,4},{14,6},{16,24},{18,... | collective-permute-start | bytes 1179656 | tf_op jit(solution)/shard_map/ppermute | solution.py:390
  120.9 16.3 %collective-permute-start.12 = (bf16[96,768]{1,0:T(8,128)(2,1)S(1)}, bf16[96,768]{1,0:T(8,128)(2,1)S(1)}, u32[]{:S(2)}, u32[]{:S(2)}) collective-permute-start(bf16[96,768]{1,0:T(8,128)(2,1)S(1)} %get-tuple-element.259), channel_id=1, source_target_pairs={{0,8},{2,10},{4,12},{6,14},{8,0},{10,2},{12,4},{14,6},{16,24},{18,... | collective-permute-start | bytes 442376 | tf_op jit(solution)/shard_map/ppermute | solution.py:390
  160.3 21.4 %collective-permute-start.34 = (bf16[2,128,768]{2,1,0:T(8,128)(2,1)S(1)}, bf16[2,128,768]{2,1,0:T(8,128)(2,1)S(1)}, u32[]{:S(2)}, u32[]{:S(2)}) collective-permute-start(bf16[2,128,768]{2,1,0:T(8,128)(2,1)S(1)} %get-tuple-element.332), channel_id=1, source_target_pairs={{0,1},{1,0},{2,3},{3,2},{4,5},{5,4},{6,7},{7,6},{8,9},{9,8},{10,11... | collective-permute-start | bytes 1179656 | tf_op jit(solution)/shard_map/ppermute | solution.py:390
  165.7 18.1 %collective-permute-start.35 = (bf16[192,768]{1,0:T(8,128)(2,1)S(1)}, bf16[192,768]{1,0:T(8,128)(2,1)S(1)}, u32[]{:S(2)}, u32[]{:S(2)}) collective-permute-start(bf16[192,768]{1,0:T(8,128)(2,1)S(1)} %combine.35.refs_0_), channel_id=1, source_target_pairs={{0,16},{2,18},{4,20},{6,22},{8,24},{10,26},{12,28},{14,30},{16,0},... | collective-permute-start | bytes 884744 | tf_op jit(solution)/shard_map/ppermute | solution.py:390
  167.7 16.2 %collective-permute-start.37 = (bf16[192,768]{1,0:T(8,128)(2,1)S(1)}, bf16[192,768]{1,0:T(8,128)(2,1)S(1)}, u32[]{:S(2)}, u32[]{:S(2)}) collective-permute-start(bf16[192,768]{1,0:T(8,128)(2,1)S(1)} %get-tuple-element.337.refs_2_), channel_id=1, source_target_pairs={{0,1},{1,0},{2,3},{3,2},{4,5},{5,4},{6,7},{7,6},{8,9},{9,8},{10,11... | collective-permute-start | bytes 884744 | tf_op jit(solution)/shard_map/ppermute | solution.py:390
  168.6 15.2 %collective-permute-start.36 = (bf16[192,768]{1,0:T(8,128)(2,1)S(1)}, bf16[192,768]{1,0:T(8,128)(2,1)S(1)}, u32[]{:S(2)}, u32[]{:S(2)}) collective-permute-start(bf16[192,768]{1,0:T(8,128)(2,1)S(1)} %get-tuple-element.325.refs_0_), channel_id=1, source_target_pairs={{0,4},{2,6},{4,0},{6,2},{8,12},{10,14},{12,8},{14,10},{16,20},{18,... | collective-permute-start | bytes 884744 | tf_op jit(solution)/shard_map/ppermute | solution.py:390
  184.0 18.5 %collective-permute-start.44 = (bf16[384,768]{1,0:T(8,128)(2,1)S(1)}, bf16[384,768]{1,0:T(8,128)(2,1)S(1)}, u32[]{:S(2)}, u32[]{:S(2)}) collective-permute-start(bf16[384,768]{1,0:T(8,128)(2,1)S(1)} %get-tuple-element.350.refs_2_), channel_id=1, source_target_pairs={{0,4},{2,6},{4,0},{6,2},{8,12},{10,14},{12,8},{14,10},{16,20},{18,... | collective-permute-start | bytes 1769480 | tf_op jit(solution)/shard_map/ppermute | solution.py:390
  184.8 17.7 %collective-permute-start.43 = (bf16[384,768]{1,0:T(8,128)(2,1)S(1)}, bf16[384,768]{1,0:T(8,128)(2,1)S(1)}, u32[]{:S(2)}, u32[]{:S(2)}) collective-permute-start(bf16[384,768]{1,0:T(8,128)(2,1)S(1)} %get-tuple-element.340.refs_0_), channel_id=1, source_target_pairs={{0,1},{1,0},{2,3},{3,2},{4,5},{5,4},{6,7},{7,6},{8,9},{9,8},{10,11... | collective-permute-start | bytes 1769480 | tf_op jit(solution)/shard_map/ppermute | solution.py:390
  202.6 31.9 %collective-permute-start.55 = (bf16[1536,768]{1,0:T(8,128)(2,1)S(1)}, bf16[1536,768]{1,0:T(8,128)(2,1)S(1)}, u32[]{:S(2)}, u32[]{:S(2)}) collective-permute-start(bf16[1536,768]{1,0:T(8,128)(2,1)S(1)} %combine.43.near_ref), channel_id=1, source_target_pairs={{0,2},{2,0},{4,6},{6,4},{8,10},{10,8},{12,14},{14,12},{16,18},{18,... | collective-permute-start | bytes 7077896 | tf_op jit(solution)/shard_map/ppermute | solution.py:390
  204.1 14.4 %collective-permute-start.50 = (bf16[128,768]{1,0:T(8,128)(2,1)S(1)}, bf16[128,768]{1,0:T(8,128)(2,1)S(1)}, u32[]{:S(2)}, u32[]{:S(2)}) collective-permute-start(bf16[128,768]{1,0:T(8,128)(2,1)S(1)} %get-tuple-element.360.refs_2_), channel_id=1, source_target_pairs={{0,8},{2,10},{4,12},{6,14},{8,0},{10,2},{12,4},{14,6},{16,24},{18,... | collective-permute-start | bytes 589832 | tf_op jit(solution)/shard_map/ppermute | solution.py:390
  218.6 13.8 %collective-permute-start.57 = (bf16[256,768]{1,0:T(8,128)(2,1)S(1)}, bf16[256,768]{1,0:T(8,128)(2,1)S(1)}, u32[]{:S(2)}, u32[]{:S(2)}) collective-permute-start(bf16[256,768]{1,0:T(8,128)(2,1)S(1)} %get-tuple-element.375.refs_2_), channel_id=1, source_target_pairs={{0,4},{2,6},{4,0},{6,2},{8,12},{10,14},{12,8},{14,10},{16,20},{18,... | collective-permute-start | bytes 1179656 | tf_op jit(solution)/shard_map/ppermute | solution.py:390
  226.3 14.1 %collective-permute-start.58 = (bf16[256,768]{1,0:T(8,128)(2,1)S(1)}, bf16[256,768]{1,0:T(8,128)(2,1)S(1)}, u32[]{:S(2)}, u32[]{:S(2)}) collective-permute-start(bf16[256,768]{1,0:T(8,128)(2,1)S(1)} %get-tuple-element.376.refs_4_), channel_id=1, source_target_pairs={{0,8},{2,10},{4,12},{6,14},{8,0},{10,2},{12,4},{14,6},{16,24},{18,... | collective-permute-start | bytes 1179656 | tf_op jit(solution)/shard_map/ppermute | solution.py:390
  245.0 14.4 %collective-permute-start.65 = (bf16[1536,768]{1,0:T(8,128)(2,1)S(1)}, bf16[1536,768]{1,0:T(8,128)(2,1)S(1)}, u32[]{:S(2)}, u32[]{:S(2)}) collective-permute-start(bf16[1536,768]{1,0:T(8,128)(2,1)S(1)} %combine.49.near_ref), channel_id=1, source_target_pairs={{0,2},{2,0},{4,6},{6,4},{8,10},{10,8},{12,14},{14,12},{16,18},{18,... | collective-permute-start | bytes 7077896 | tf_op jit(solution)/shard_map/ppermute | solution.py:390
  (58 other events, 500.4 us)
